TPU v7x, 32 devices: a whole 2x2x4 slice. The times are simulated.
32 devices in a mesh: dp: 4 (over y, x), seq: 8 (over z, core).
Axes of the slice: x: 2, y: 2, z: 4, core: 2. Of those that a mesh axis runs over, the one named last changes fastest.
Arguments:
- tokens: bfloat16 [2, 4, 1024, 768], P(None, 'dp', 'seq'), may hold values from -6 to 6
- cotangent: bfloat16 [2, 4, 1024, 768], P(None, 'dp', 'seq'), may hold values from -6 to 6
- expert_ids: int32 [2, 4, 1024, 2], P(None, 'dp', 'seq'), may hold values from 0 to 15, all different within a row; in each aligned block of 128 rows (0 to 127, 128 to 255, ..., all dimensions but the last counted through in order) at most 18 rows name the same one
- buckets: int32 [1024], replicated, may hold values from 0 to 31
- gain_attn: bfloat16 [768], P(('dp', 'seq')), may hold values from 0.5 to 1.5
- w_qkv: bfloat16 [768, 2304], P(('dp', 'seq')), may hold values from -0.21875 to 0.21875
- rel_bias: bfloat16 [32, 12], replicated, may hold values from -4 to 4
- w_attn_out: bfloat16 [768, 768], P(('dp', 'seq')), may hold values from -2 to 2
- gain_moe: bfloat16 [768], P(('dp', 'seq')), may hold values from 0.5 to 1.5
- router: bfloat16 [768, 16], P(('dp', 'seq')), may hold values from -0.15625 to 0.15625
- w_up: bfloat16 [16, 768, 3072], P('seq', None, 'dp'), may hold values from -0.21875 to 0.21875
- w_down: bfloat16 [16, 768, 3072], P('seq', None, 'dp'), may hold values from -0.109375 to 0.109375
Outputs:
- mixed_out: bfloat16 [2, 4, 1024, 768], P(None, 'dp', 'seq')
- grad_tokens: bfloat16 [2, 4, 1024, 768], P(None, 'dp', 'seq')
- grad_gain_attn: float32 [768], P(('dp', 'seq'))
- grad_qkv: float32 [768, 2304], P(('dp', 'seq'))
- grad_rel_bias: float32 [32, 12], replicated
- grad_attn_out: float32 [768, 768], P(('dp', 'seq'))
- grad_gain_moe: float32 [768], P(('dp', 'seq'))
- grad_router: float32 [768, 16], P(('dp', 'seq'))
- grad_up: float32 [16, 768, 3072], P('seq', None, 'dp')
- grad_down: float32 [16, 768, 3072], P('seq', None, 'dp')
Inputs may be any that keep to these rules, and one draw needn't show every extreme that they name: `expert_ids`: the two ids of a token differ. In each aligned block of 128 positions of one sequence (the positions of one device), no expert is chosen more than 18 times, and in some blocks one expert is chosen exactly 18 times; every expert is chosen somewhere.
All inputs are finite; a program needn't handle non-finite values.
Results may differ from a plain program's by a relative error of at most 0.02.
Values may be sent and summed in bfloat16 or wider, within the bound.
No kernel may reach another device: no remote copies, remote signals or barrier semaphores. Data moves between devices by JAX's collectives and lax.ppermute only.
A program may use at most 192 MiB of HBM per device.

v0:
```python
import functools
import math

import jax
import jax.numpy as jnp
from jax import lax
from jax.experimental import pallas as pl
from jax.experimental.pallas import tpu as pltpu
from jax.sharding import Mesh
from jax.sharding import PartitionSpec as P

HD = 64
LANES = 128
EPS = 1e-06
NEG = -1e30
F32 = jnp.float32
BF16 = jnp.bfloat16
VMEM_BYTES = 56 * 1024 * 1024
INV_SQRT2 = 1.0 / math.sqrt(2.0)
INV_SQRT2PI = 1.0 / math.sqrt(2.0 * math.pi)


def mm(a, b):
    return lax.dot_general(a, b, (((1,), (0,)), ((), ())), preferred_element_type=F32)


def mm_nt(a, b):
    return lax.dot_general(a, b, (((1,), (1,)), ((), ())), preferred_element_type=F32)


def mm_tn(a, b):
    return lax.dot_general(a, b, (((0,), (0,)), ((), ())), preferred_element_type=F32)


def iota(shape, dim):
    return lax.broadcasted_iota(jnp.int32, shape, dim)


def split3(v):
    hi = v.astype(BF16).astype(F32)
    rest = v - hi
    mid = rest.astype(BF16).astype(F32)
    return hi, mid, rest - mid


def call(kernel, outs, ins, scratch=(), smem=0, name=None, after=()):
    spec = [pl.BlockSpec(memory_space=pltpu.SMEM)] * smem
    spec += [pl.BlockSpec(memory_space=pltpu.VMEM)] * (len(ins) - smem)
    spec += [pl.BlockSpec(memory_space=pl.ANY)] * len(after)
    count = len(ins)

    def body(*refs):
        kernel(*refs[:count], *refs[count + len(after) :])

    return pl.pallas_call(
        body,
        out_shape=[jax.ShapeDtypeStruct(s, d) for s, d in outs],
        in_specs=spec,
        out_specs=[pl.BlockSpec(memory_space=pltpu.VMEM)] * len(outs),
        scratch_shapes=list(scratch),
        compiler_params=pltpu.CompilerParams(vmem_limit_bytes=VMEM_BYTES),
        cost_estimate=pl.CostEstimate(flops=0, transcendentals=0, bytes_accessed=1),
        name=name,
    )(*ins, *after)


def route_kernel(dims, meta_ref, ids_ref, cot_ref, slot_ref, out_ref):
    rows, experts, local, seq, cp = dims
    ids = ids_ref[...]
    expert = iota((rows, experts), 1)
    hot = [(ids[:, j : j + 1] == expert).astype(F32) for j in range(2)]
    before = (iota((rows, rows), 0) > iota((rows, rows), 1)).astype(BF16)
    rank = mm(before, (hot[0] + hot[1]).astype(BF16))
    cols = []
    for j in range(2):
        own = jnp.sum(hot[j] * rank, axis=1, keepdims=True).astype(jnp.int32)
        e = ids[:, j : j + 1]
        cols.append(((e % local) ^ meta_ref[3]) * (seq * cp) + (e // local) * cp + own)
    lane = iota((rows, LANES), 1)
    slot_ref[...] = jnp.where(lane == 0, cols[0], cols[1])
    place = place_both([merged(col, cp, seq * cp) for col in cols], 0, 2 * seq * cp)
    out_ref[...] = mm_tn(place, cot_ref[...]).astype(BF16)


def merged(col, cp, per_expert):
    inside = col % per_expert
    return inside // cp * (2 * cp) + col // per_expert * cp + inside % cp


def place_one(col, e, count):
    return (iota((col.shape[0], count), 1) + e * count == col).astype(BF16)


def place_both(cols, e, count):
    where = iota((cols[0].shape[0], count), 1) + e * count
    return jnp.logical_or(where == cols[0], where == cols[1]).astype(BF16)


def attn_fwd_kernel(dims, meta_ref, *refs):
    half, dp, hpd, block, gain_lane, scale = dims
    own, sib, wp = refs[:half], refs[half : 2 * half], refs[2 * half : 2 * half + dp]
    brev_ref = refs[2 * half + dp]
    o_ref, qkv_ref, xn_ref, w_ref, lse_ref, slab_ref, gain_ref = refs[2 * half + dp + 1 :]
    z, c, d = meta_ref[0], meta_ref[1], meta_ref[2]
    part = wp[0].shape[0]
    for j in range(dp):
        w_ref[pl.ds(pl.multiple_of((d ^ j) * part, part), part), :] = wp[j][...]
    tile = 3 * hpd * HD // LANES * LANES
    turned = jnp.transpose(w_ref[:, tile : tile + LANES].astype(F32))
    gain = turned[gain_lane : gain_lane + 1, :]
    gain_ref[...] = gain
    rows = own[0].shape[0]
    for group, core in ((own, c), (sib, 1 - c)):
        for k in range(half):
            x = group[k][...].astype(F32)
            r = lax.rsqrt(jnp.mean(x * x, axis=1, keepdims=True) + EPS)
            start = pl.multiple_of((2 * (z ^ k) + core) * rows, rows)
            xn_ref[pl.ds(start, rows), :] = (x * r * gain).astype(BF16)
    length = xn_ref.shape[0]
    for i in range(length // block):
        part_rows = slice(i * block, (i + 1) * block)
        qkv_ref[part_rows, :] = mm(xn_ref[part_rows, :], w_ref[...]).astype(BF16)
    span = length + block
    width_h = hpd * HD
    for h in range(hpd):
        base = brev_ref[h : h + 1, :]
        rolled = [base if i == 7 else pltpu.roll(base, span - (7 - i), 1) for i in range(8)]
        slab = jnp.concatenate(rolled, axis=0)
        n = 8
        while n < block:
            slab = jnp.concatenate([pltpu.roll(slab, span - n, 1), slab], axis=0)
            n *= 2
        slab_ref[h] = slab[:, :length]
    lane = iota((block, LANES), 1)
    for i in range(length // block):
        q_rows = slice(i * block, (i + 1) * block)
        keys = (i + 1) * block
        lse = jnp.zeros((block, LANES), F32)
        for h in range(hpd):
            q = qkv_ref[q_rows, h * HD : (h + 1) * HD] * jnp.asarray(scale, BF16)
            k = qkv_ref[:keys, width_h + h * HD : width_h + (h + 1) * HD]
            v = qkv_ref[:keys, 2 * width_h + h * HD : 2 * width_h + (h + 1) * HD]
            s = mm_nt(q, k) + slab_ref[h, :, length - keys :]
            top = jnp.max(s, axis=1, keepdims=True)
            e = jnp.exp(s - top)
            total = jnp.sum(e, axis=1, keepdims=True)
            p = (e * (1.0 / total)).astype(BF16)
            o_ref[q_rows, h * HD : (h + 1) * HD] = mm(p, v).astype(BF16)
            lse = jnp.where(lane == h, top + jnp.log(total), lse)
        lse_ref[q_rows, :] = lse


def three_parts(table, width):
    wide = jnp.concatenate(list(split3(table)), axis=1)
    if width > 3 * LANES:
        wide = jnp.concatenate([wide, jnp.zeros((8, width - 3 * LANES), F32)], axis=1)
    return jnp.concatenate([wide, jnp.zeros_like(wide)], axis=0).astype(BF16)


def attn_bwd_kernel(dims, meta_ref, do_ref, qkv_ref, w_ref, lse_ref, slab_ref, *refs):
    half, hpd, block, scale, buckets = dims
    hot_ref, dx_own, dx_sib, dqkv_ref, table_ref, dk_ref, dv_ref, db_ref, gb_ref = refs
    gb_ref[...] = jnp.zeros_like(gb_ref)
    z, c = meta_ref[0], meta_ref[1]
    length = qkv_ref.shape[0]
    width_h = hpd * HD
    blocks = length // block
    dqkv_ref[...] = jnp.zeros_like(dqkv_ref)
    for h in range(hpd):
        cols = slice(h * HD, (h + 1) * HD)
        k_cols = slice(width_h + h * HD, width_h + (h + 1) * HD)
        v_cols = slice(2 * width_h + h * HD, 2 * width_h + (h + 1) * HD)
        for i in range(blocks - 1, -1, -1):
            rows = slice(i * block, (i + 1) * block)
            keys = (i + 1) * block
            q = qkv_ref[rows, cols] * jnp.asarray(scale, BF16)
            k = qkv_ref[:keys, k_cols]
            v = qkv_ref[:keys, v_cols]
            do = do_ref[rows, cols]
            s = mm_nt(q, k) + slab_ref[h, :, length - keys :]
            p = jnp.exp(s - lse_ref[rows, h : h + 1])
            dprob = mm_nt(do, v)
            delta = jnp.sum(p * dprob, axis=1, keepdims=True)
            ds32 = p * (dprob - delta)
            ds = ds32.astype(BF16)
            dqkv_ref[rows, cols] = (mm(ds, k) * scale).astype(BF16)
            dk = mm_tn(ds, q)
            dv = mm_tn(p.astype(BF16), do)
            if i == blocks - 1:
                dk_ref[...] = dk
                dv_ref[...] = dv
                db_ref[:, :length] = ds.astype(F32)
            else:
                dk_ref[:keys, :] += dk
                dv_ref[:keys, :] += dv
                db_ref[:, length - keys : length] += ds.astype(F32)
        dqkv_ref[:, k_cols] = dk_ref[...].astype(BF16)
        dqkv_ref[:, v_cols] = dv_ref[...].astype(BF16)
        db_ref[:, length:] = jnp.zeros((block, block), F32)
        n = block
        acc = db_ref[...]
        while n > 1:
            n //= 2
            acc = pltpu.roll(acc[:n], n, 1) + acc[n:]
        gb_ref[h : h + 1, :] = acc
    hot = hot_ref[...]
    hi, mid, low = split3(gb_ref[...])
    by_bucket = mm(hi.astype(BF16), hot) + mm(mid.astype(BF16), hot) + mm(low.astype(BF16), hot)
    table = jnp.zeros((8, LANES), F32)
    row, lane = iota((8, LANES), 0), iota((8, LANES), 1)
    for h in range(hpd):
        head = meta_ref[4] * hpd + h
        here = jnp.logical_and(row == head % 8, lane // buckets == head // 8)
        table = jnp.where(here, by_bucket[h : h + 1, :], table)
    table_ref[...] = table
    rows = dx_own.shape[1]
    w = w_ref[...]
    for out_ref, core in ((dx_own, c), (dx_sib, 1 - c)):
        for k in range(half):
            start = pl.multiple_of((2 * (z ^ k) + core) * rows, rows)
            out_ref[k] = mm_nt(dqkv_ref[pl.ds(start, rows), :], w).astype(BF16)


def cols_kernel(dims, meta_ref, xn_ref, dqkv_ref, table_ref, *refs):
    gq_refs, gq_ref = refs[:-1], refs[-1]
    gq_ref[...] = mm_tn(xn_ref[...], dqkv_ref[...]).astype(BF16)
    table = three_parts(table_ref[...], gq_ref.shape[1])
    part = gq_refs[0].shape[0] - 16
    for j, piece in enumerate(gq_refs):
        start = pl.multiple_of((meta_ref[2] ^ j) * part, part)
        piece[:part, :] = gq_ref[pl.ds(start, part), :]
        piece[part:, :] = table


def pick_probs(ids, probs):
    expert = iota(probs.shape, 1)
    hot = [(ids[:, j : j + 1] == expert).astype(F32) for j in range(2)]
    picked = [jnp.sum(probs * one, axis=1, keepdims=True) for one in hot]
    total = picked[0] + picked[1]
    return hot, total, [one / total for one in picked]


def norm_parts(x1):
    r = lax.rsqrt(jnp.mean(x1 * x1, axis=1, keepdims=True) + EPS)
    return r, x1 * r


def head_rows(groups, width_h, width):
    return [(g, min(width_h, width - g * width_h)) for g in range(groups) if g * width_h < width]


def mid_kernel(dims, o_ref, x_ref, ids_ref, slot_ref, *refs):
    seqs, groups, cp, dead, per_expert, experts = dims
    ws_ref, x1_ref, xn_ref, prob_ref, gain_ref, send_ref = refs
    width = x_ref.shape[1]
    lane_at = width + experts
    tile = lane_at // LANES * LANES
    turned = jnp.transpose(ws_ref[:, tile : tile + LANES].astype(F32))
    gain = turned[lane_at - tile : lane_at - tile + 1, :]
    gain_ref[...] = gain
    rows = x_ref.shape[0] // seqs
    width_h = o_ref.shape[2]
    for m in range(seqs):
        part = slice(m * rows, (m + 1) * rows)
        acc = x_ref[part, :].astype(F32)
        for g, count in head_rows(groups, width_h, width):
            w_rows = ws_ref[g * width_h : g * width_h + count, :width]
            acc += mm(o_ref[m * groups + g][:, :count], w_rows)
        x1_ref[part, :] = acc
    r, u = norm_parts(x1_ref[...])
    xn = (u * gain).astype(BF16)
    xn_ref[...] = xn
    logits = mm(xn, ws_ref[:, width : width + experts])
    e = jnp.exp(logits - jnp.max(logits, axis=1, keepdims=True))
    probs = e / jnp.sum(e, axis=1, keepdims=True)
    prob_ref[...] = probs
    ids = ids_ref[...]
    _, _, gates = pick_probs(ids, probs)
    cols = [slot_ref[:, j : j + 1] for j in range(2)]
    lane = iota((xn.shape[0], LANES), 1)
    places = [merged(col, cp, per_expert) for col in cols]
    out = mm_tn(place_both(places, 0, 2 * per_expert), xn)
    extra = jnp.zeros((2 * per_expert, LANES), F32)
    for j in range(2):
        rank = cols[j] % cp
        hi, mid, low = split3(gates[j])
        value = jnp.where(lane < cp, hi, jnp.where(lane < 2 * cp, mid, low))
        keep = jnp.logical_and(lane % cp == rank, lane < 3 * cp)
        carried = jnp.where(keep, value, 0.0).astype(BF16)
        extra += mm_tn(place_one(places[j] - rank + dead, 0, 2 * per_expert), carried)
    send_ref[:, LANES:] = out[:, LANES:].astype(BF16)
    send_ref[:, :LANES] = (out[:, :LANES] + extra).astype(BF16)


def expert_kernel(dims, *refs):
    count, cp, dead = dims
    xs, cs = refs[:count], refs[count : 2 * count]
    weights = refs[2 * count : 2 * count + 4]
    outs = refs[2 * count + 4 :]
    dx_refs = outs[:count]
    h_refs, dpre_refs, dy_ref = outs[count : count + 2], outs[count + 2 : count + 4], outs[count + 4]
    rows = xs[0].shape[0]
    chunks = rows // cp
    lane = iota((rows, LANES), 1)
    row = iota((rows, LANES), 0)
    take = (iota((chunks, rows), 1) == iota((chunks, rows), 0) * cp + dead).astype(BF16)
    spread = (iota((rows, chunks), 0) // cp == iota((rows, chunks), 1)).astype(BF16)
    mine = jnp.logical_and(lane % cp == row % cp, lane < 3 * cp)
    mine_first = lane == row % cp
    target = iota((rows, rows), 1) // cp * cp + dead
    put_hi = (iota((rows, rows), 0) == target).astype(BF16)
    put_low = (iota((rows, rows), 0) == target + 1).astype(BF16)
    for j in range(count):
        part = slice(j * rows, (j + 1) * rows)
        x = xs[j][...]
        cot = cs[j][...]
        carried = mm(spread, mm(take, x[:, :LANES]).astype(BF16))
        gate = jnp.sum(jnp.where(mine, carried, 0.0), axis=1, keepdims=True)
        dy_ref[part, :] = (cot.astype(F32) * gate).astype(BF16)
        dg = jnp.zeros((rows, 1), F32)
        dx = jnp.zeros((rows, x.shape[1]), F32)
        for f in range(2):
            pre = mm(x, weights[2 * f][...])
            cdf = 0.5 * (1.0 + lax.erf(pre * INV_SQRT2))
            hidden = pre * cdf
            h_refs[f][part, :] = hidden.astype(BF16)
            slope = cdf + pre * (jnp.exp(-0.5 * pre * pre) * INV_SQRT2PI)
            dh = mm(cot, weights[2 * f + 1][...])
            dg += jnp.sum(hidden * dh, axis=1, keepdims=True)
            dpre = (dh * slope * gate).astype(BF16)
            dpre_refs[f][part, :] = dpre
            dx += mm_nt(dpre, weights[2 * f][...])
        dg_hi = dg.astype(BF16).astype(F32)
        extra = mm(put_hi, jnp.where(mine_first, dg_hi, 0.0).astype(BF16))
        extra += mm(put_low, jnp.where(mine_first, dg - dg_hi, 0.0).astype(BF16))
        dx_refs[j][:, LANES:] = dx[:, LANES:].astype(BF16)
        dx_refs[j][:, :LANES] = (dx[:, :LANES] + extra).astype(BF16)


def up_grad_kernel(dims, *refs):
    calls, count = dims
    xs, dpre, out_ref = refs[: calls * count], refs[calls * count : -1], refs[-1]
    rows = xs[0].shape[0]
    acc = None
    for i in range(calls):
        for j in range(count):
            term = mm_tn(xs[i * count + j][...], dpre[i][j * rows : (j + 1) * rows, :])
            acc = term if acc is None else acc + term
    out_ref[...] = acc.astype(out_ref.dtype)


def expert_out_kernel(dims, *refs):
    calls, count = dims
    hidden, weights, outs = refs[: 2 * calls], refs[2 * calls : 2 * calls + 2], refs[2 * calls + 2 :]
    rows = outs[0].shape[0]
    for i in range(calls):
        for j in range(count):
            part = slice(j * rows, (j + 1) * rows)
            y = mm_nt(hidden[2 * i][part, :], weights[0][...])
            y += mm_nt(hidden[2 * i + 1][part, :], weights[1][...])
            outs[i * count + j][...] = y.astype(BF16)


def down_grad_kernel(dims, *refs):
    calls = dims
    saved, outs = refs[: 3 * calls], refs[3 * calls :]
    for f in range(2):
        acc = mm_tn(saved[2][...], saved[f][...])
        for i in range(1, calls):
            acc += mm_tn(saved[3 * i + 2][...], saved[3 * i + f][...])
        outs[f][...] = acc.astype(outs[f].dtype)


def both_experts_kernel(dims, meta_ref, up_ref, up_pair, down_ref, down_pair, out_up, out_down):
    bit = meta_ref[3]
    for own, pair, out in ((up_ref, up_pair, out_up), (down_ref, down_pair, out_down)):
        out[bit] = own[...]
        out[1 - bit] = pair[1 - bit].astype(F32)


def merge_kernel(dims, *refs):
    dp, shard = dims
    lines, smalls, out_ref, acc_ref = refs[:dp], refs[dp : 2 * dp], refs[2 * dp], refs[2 * dp + 1]
    part = smalls[0].shape[0]
    cols = lines[0].shape[1]
    table = jnp.zeros((8, LANES), F32)
    acc = jnp.zeros((part, cols), F32)
    small = jnp.zeros(smalls[0].shape, F32)
    for j in range(dp):
        acc += lines[j][:part, :].astype(F32)
        tail = lines[j][part:, :].astype(F32)[:8]
        table += sum(tail[:, i * LANES : (i + 1) * LANES] for i in range(3))
        small += smalls[j][...].astype(F32)
    acc_ref[:, :cols] = acc
    acc_ref[:, cols:] = small
    width = acc_ref.shape[1]
    rows = out_ref.shape[1]
    tail = jnp.concatenate(list(split3(table)), axis=1)
    tail = jnp.concatenate([tail, jnp.zeros((8, width - 3 * LANES), F32)], axis=1)
    fill = rows - 8 - shard
    for s in range(out_ref.shape[0]):
        block = [acc_ref[s * shard : (s + 1) * shard, :], tail]
        if fill:
            block = [block[0], jnp.zeros((fill, width), F32), tail]
        out_ref[s] = jnp.concatenate(block, axis=0).astype(BF16)


def finish_kernel(dims, got_ref, w_ref, gain_ref, *outs):
    seqs, groups, hpd, cols, experts = dims
    qkv_ref, out_ref, router_ref, first_ref, second_ref, table_ref = outs
    width_h = hpd * HD
    shard, width = w_ref.shape[0], w_ref.shape[1] // 3
    got = [got_ref[s].astype(F32) for s in range(seqs * groups)]
    whole = functools.reduce(jnp.add, got)
    last = whole.shape[0] - 8
    table_ref[...] = sum(whole[last:, i * LANES : (i + 1) * LANES] for i in range(3))
    small = whole[:shard, cols:]
    out_ref[...] = small[:, :width]
    router_ref[...] = small[:, width : width + experts]
    tile = (width + experts) // LANES * LANES
    turned = jnp.transpose(pad_rows(small[:, tile : tile + LANES]))
    second_ref[...] = turned[width + experts - tile :][:1, :shard]
    for g, count in head_rows(groups, width_h, width):
        acc = functools.reduce(jnp.add, [got[m * groups + g][:shard, :cols] for m in range(seqs)])
        for i in range(3):
            start = i * width + g * width_h
            qkv_ref[:, start : start + count] = acc[:, i * width_h : i * width_h + count]
    total = jnp.sum(qkv_ref[...] * w_ref[...].astype(F32), axis=1, keepdims=True)
    total = jnp.broadcast_to(total / gain_ref[...].astype(F32), (shard, LANES))
    first_ref[...] = jnp.transpose(pad_rows(total))[:1, :shard]


def pad_rows(value):
    count = LANES - value.shape[0]
    return jnp.concatenate([value, jnp.zeros((count, value.shape[1]), F32)], axis=0)


def add_kernel(dims, *refs):
    cp, dead = dims
    parts, out_ref = refs[:-1], refs[-1]
    acc = parts[0][...].astype(F32)
    for part in parts[1:]:
        acc += part[...].astype(F32)
    if dead is None:
        out_ref[...] = acc.astype(BF16)
        return
    out_ref[:, LANES:] = acc[:, LANES:].astype(BF16)
    first = acc[:, :LANES]
    rows = first.shape[0]
    place = iota((rows, LANES), 0) % cp
    both = first + pltpu.roll(first, rows - 1, 0)
    high = both.astype(BF16).astype(F32)
    low = pltpu.roll(both - high, 1, 0)
    out = jnp.where(place == dead, high, jnp.where(place == dead + 1, low, first))
    out_ref[:, :LANES] = out.astype(BF16)


def add_both_kernel(dims, *refs):
    count = (len(refs) - 2) // 2
    for i in range(2):
        acc = refs[i * count][...].astype(F32)
        for part in refs[i * count + 1 : (i + 1) * count]:
            acc += part[...].astype(F32)
        refs[2 * count + i][...] = acc.astype(BF16)


def back_kernel(dims, *refs):
    seqs, groups, cp, dead, per_expert, local = dims
    rets = refs[:local]
    x1_ref, prob_ref, ids_ref, slot_ref, cot_ref = refs[local : local + 5]
    ws_ref, gain_ref = refs[local + 5 : local + 7]
    dx1_ref, da_ref, do_ref, dl_ref, prod_ref = refs[local + 7 :]
    width = x1_ref.shape[1]
    ids = ids_ref[...]
    probs = prob_ref[...]
    hot, total, gates = pick_probs(ids, probs)
    cols = [slot_ref[:, j : j + 1] for j in range(2)]
    rows = ids.shape[0]
    lane = iota((rows, LANES), 1)
    ranks = [col % cp for col in cols]
    moe = jnp.zeros(x1_ref.shape, F32)
    heads = [jnp.zeros((rows, LANES), F32) for _ in range(2)]
    for k in range(local):
        ret = rets[k][...]
        moe += mm(place_both(cols, k, per_expert), ret)
        for j in range(2):
            base = cols[j] - ranks[j] + dead
            heads[j] += mm(place_both([base, base + 1], k, per_expert), ret[:, :LANES])
    dg = [
        jnp.sum(jnp.where(lane == ranks[j], heads[j], 0.0), axis=1, keepdims=True) for j in range(2)
    ]
    mean_dg = dg[0] * gates[0] + dg[1] * gates[1]
    dprob = hot[0] * ((dg[0] - mean_dg) / total) + hot[1] * ((dg[1] - mean_dg) / total)
    dl = probs * (dprob - jnp.sum(probs * dprob, axis=1, keepdims=True))
    dl_ref[...] = dl
    router = ws_ref[:, width : width + probs.shape[1]]
    dl_hi = dl.astype(BF16)
    dl_low = (dl - dl_hi.astype(F32)).astype(BF16)
    dxn = moe + mm_nt(dl_hi, router) + mm_nt(dl_low, router)
    r, u = norm_parts(x1_ref[...])
    prod_ref[...] = (dxn * u).astype(BF16)
    scaled = dxn * gain_ref[...]
    dx1 = cot_ref[...].astype(F32) + r * (
        scaled - u * jnp.mean(u * scaled, axis=1, keepdims=True)
    )
    dx1_ref[...] = dx1
    da = dx1.astype(BF16)
    da_ref[...] = da
    width_h = do_ref.shape[2]
    each = rows // seqs
    used = head_rows(groups, width_h, width)
    if len(used) < groups or used[-1][1] < width_h:
        do_ref[...] = jnp.zeros_like(do_ref)
    for g, count in used:
        block = mm_nt(da, ws_ref[g * width_h : g * width_h + count, :width]).astype(BF16)
        for m in range(seqs):
            do_ref[m * groups + g, :, :count] = block[m * each : (m + 1) * each, :]


def side_kernel(dims, first_ref, second_ref, out_ref):
    both = [first_ref[...].astype(F32), second_ref[...].astype(F32)]
    out_ref[...] = jnp.concatenate(both, axis=1).astype(BF16)


def pair_kernel(dims, own_ref, got_ref, *outs):
    for k, out_ref in enumerate(outs):
        out_ref[...] = (own_ref[k].astype(F32) + got_ref[k].astype(F32)).astype(BF16)


def small_grad_kernel(dims, meta_ref, o_ref, da_ref, xn_ref, dl_ref, prod_ref, *refs):
    seqs, groups = dims
    pieces, out_ref = refs[:-1], refs[-1]
    width_h = o_ref.shape[2]
    rows, width = da_ref.shape
    each = rows // seqs
    experts = dl_ref.shape[1]
    for g, count in head_rows(groups, width_h, width):
        acc = jnp.zeros((width_h, width), F32)
        for m in range(seqs):
            acc += mm_tn(o_ref[m * groups + g], da_ref[m * each : (m + 1) * each, :])
        out_ref[g * width_h : g * width_h + count, :width] = acc[:count].astype(BF16)
    dl = dl_ref[...]
    dl_hi = dl.astype(BF16)
    dl_low = (dl - dl_hi.astype(F32)).astype(BF16)
    xn = xn_ref[...]
    tail = out_ref.shape[1] - width
    cut = (iota((experts, tail), 0) == iota((experts, tail), 1)).astype(BF16)
    router_part = mm_tn(xn, mm(dl_hi, cut).astype(BF16)) + mm_tn(xn, mm(dl_low, cut).astype(BF16))
    ones = (iota((rows, tail), 1) == experts).astype(BF16)
    out_ref[:, width:] = (router_part + mm_tn(prod_ref[...], ones)).astype(BF16)
    part = pieces[0].shape[0]
    for j, piece in enumerate(pieces):
        start = pl.multiple_of((meta_ref[2] ^ j) * part, part)
        piece[...] = out_ref[pl.ds(start, part), :]


def mixed_kernel(dims, *refs):
    per_expert, local = dims
    rets = refs[:local]
    x1_ref, prob_ref, ids_ref, slot_ref, out_ref = refs[local:]
    _, _, gates = pick_probs(ids_ref[...], prob_ref[...])
    out = x1_ref[...]
    for j in range(2):
        col = slot_ref[:, j : j + 1]
        y = mm(place_one(col, 0, per_expert), rets[0][...])
        for k in range(1, local):
            y += mm(place_one(col, k, per_expert), rets[k][...])
        out += gates[j] * y
    out_ref[...] = out.astype(BF16)


def last_kernel(dims, meta_ref, *refs):
    half, seqs, groups = dims
    parts = refs[:half]
    x_ref, dx1_ref, gain_ref, out_ref, acc_ref = refs[half:]
    z = meta_ref[0]
    rows = parts[0].shape[0]
    acc_ref[...] = jnp.zeros_like(acc_ref)
    for k in range(half):
        m = (2 * (z ^ k)) // groups
        acc_ref[m] += parts[k][...].astype(F32)
    gain = gain_ref[...]
    for m in range(seqs):
        part = slice(m * rows, (m + 1) * rows)
        x = x_ref[part, :].astype(F32)
        r = lax.rsqrt(jnp.mean(x * x, axis=1, keepdims=True) + EPS)
        u = x * r
        scaled = acc_ref[m] * gain
        back = r * (scaled - u * jnp.mean(u * scaled, axis=1, keepdims=True))
        out_ref[part, :] = (dx1_ref[part, :] + back).astype(BF16)


DP = ("hi", "lo")


def permute_xor(value, axis, offset):
    axis = DP if axis == "dp" else axis
    count = lax.axis_size(axis)
    return lax.ppermute(value, axis, [(i, i ^ offset) for i in range(count)])


def spread_dp(value):
    return [value] + [permute_xor(value, "dp", j) for j in range(1, lax.axis_size(DP))]


def swap_seq(value):
    return lax.all_to_all(value, "seq", split_axis=0, concat_axis=0, tiled=True)


def shards(
    tokens,
    cotangent,
    expert_ids,
    buckets,
    gain_attn,
    w_qkv,
    rel_bias,
    w_attn_out,
    gain_moe,
    router,
    w_up,
    w_down,
):
    micro, batch, rows, width = tokens.shape
    heads = width // HD
    seqs = micro * batch
    seq, dp = lax.axis_size("seq"), lax.axis_size(DP)
    half = seq // 2
    length = seq * rows
    groups = seq // seqs
    hpd = -(-heads // groups)
    width_h = hpd * HD
    padded_heads = hpd * groups
    total = seqs * rows
    experts, local = router.shape[1], w_up.shape[0]
    slots = seqs * (expert_ids.shape[3] * rows // experts + 2)
    cp = -(-(slots + 2) // 8) * 8
    per_expert = seq * cp
    block = 256
    scale = 1.0 / math.sqrt(HD)
    shard = w_qkv.shape[0]
    me, dpi = lax.axis_index("seq"), lax.axis_index(DP)
    z, c = me // 2, me % 2
    low = dp // 2
    my_group = me % groups
    meta = jnp.stack([z, c, dpi, dpi // low, my_group]).astype(jnp.int32)

    x_flat = tokens.reshape(seqs, rows, width)
    cot_flat = cotangent.reshape(total, width)
    ids_flat = expert_ids.reshape(total, expert_ids.shape[3])

    own, sib = [], []
    for k in range(half):
        target = (2 * (z ^ k)) // groups
        piece = lax.dynamic_index_in_dim(x_flat, target, 0, keepdims=False)
        if k:
            piece = permute_xor(piece, "seq", 2 * k)
        own.append(piece)
        sib.append(permute_xor(piece, "seq", 1))

    gain_lane = (3 * width_h) % LANES
    cols = max(3 * width_h - gain_lane + LANES, 3 * LANES)
    w_four = w_qkv.reshape(shard, 3, heads, HD)
    w_four = jnp.pad(w_four, ((0, 0), (0, 0), (0, padded_heads - heads), (0, 0)))
    w_groups = jnp.transpose(w_four.reshape(shard, 3, groups, width_h), (2, 0, 1, 3))
    w_groups = w_groups.reshape(groups, shard, 3 * width_h)
    gain_col = jnp.broadcast_to(gain_attn[None, :, None], (groups, shard, 1))
    w_groups = jnp.concatenate([w_groups, gain_col], axis=2)
    w_groups = jnp.pad(w_groups, ((0, 0), (0, 0), (0, cols - 3 * width_h - 1)))

    w_small = jnp.concatenate([w_attn_out, router, gain_moe[:, None]], axis=1)
    small_cols = -(-w_small.shape[1] // LANES) * LANES
    w_small = jnp.pad(w_small, ((0, 0), (0, small_cols - w_small.shape[1])))
    w_small = lax.all_gather(w_small, DP + ("seq",), axis=0, tiled=True)
    w_line = swap_seq(jnp.tile(w_groups, (seqs, 1, 1))).reshape(seq * shard, cols)
    w_parts = spread_dp(w_line)

    hot = (buckets[:, None] == jnp.arange(rel_bias.shape[0], dtype=jnp.int32)).astype(F32)
    repeat = LANES // rel_bias.shape[0]
    hot_rev = jnp.pad(jnp.tile(jnp.flip(hot, axis=0), (1, repeat)), ((0, block), (0, 0)))
    hot_rev = hot_rev.astype(BF16)
    table = jnp.pad(rel_bias.astype(F32), ((0, 0), (0, padded_heads - heads)))
    table = lax.dynamic_slice_in_dim(table, my_group * hpd, hpd, 1)
    by_distance = jnp.einsum("tn,nh->ht", hot, table, precision=lax.Precision.HIGHEST)
    bias_rev = jnp.concatenate(
        [jnp.flip(by_distance, axis=1), jnp.full((hpd, block), NEG, F32)], axis=1
    )

    slot_cols, cot_send = call(
        functools.partial(route_kernel, (total, experts, local, seq, cp)),
        [
            ((total, LANES), jnp.int32),
            ((2 * per_expert, width), BF16),
        ],
        [meta, ids_flat, cot_flat],
        smem=1,
        name="route",
        after=own[1:] + sib + w_parts,
    )

    def to_experts(value):
        got = swap_seq(value.reshape(seq, 2 * cp, width)).reshape(seq, 2, cp, width)
        first, second = (got[:, k].reshape(per_expert, width) for k in range(2))
        second = permute_xor(second, "dp", low)
        return [
            [item] + [permute_xor(item, "dp", j) for j in range(1, low)]
            for item in (first, second)
        ]

    cot_parts = to_experts(cot_send)
    ff = w_up.shape[2]
    away = 1 - dpi // low
    away_pair = jnp.stack(
        [lax.dynamic_index_in_dim(item, away, 0, keepdims=False) for item in (w_up, w_down)]
    )
    away_pair = lax.all_gather(away_pair, "hi", axis=0)
    away_got = lax.dynamic_index_in_dim(away_pair, away, 0, keepdims=False)
    up_got, down_got = away_got[0], away_got[1]
    up_own, down_own = (
        lax.dynamic_index_in_dim(item, 1 - away, 0, keepdims=False) for item in (w_up, w_down)
    )

    def from_experts(pieces):
        return [pieces[0]] + [permute_xor(pieces[j], "dp", j) for j in range(1, low)]

    o_all, qkv, xn1, w_mine, lse, slab, gain_first = call(
        functools.partial(attn_fwd_kernel, (half, dp, hpd, block, gain_lane, scale)),
        [
            ((length, width_h), BF16),
            ((length, cols), BF16),
            ((length, width), BF16),
            ((width, cols), BF16),
            ((length, LANES), F32),
            ((hpd, block, length), F32),
            ((1, width), F32),
        ],
        [meta] + own + sib + w_parts + [bias_rev],
        smem=1,
        name="attn_fwd",
        after=[cot_send, hot_rev],
    )
    o_mine = swap_seq(o_all.reshape(seq, rows, width_h))
    x1, xn2, probs, gain_second, send = call(
        functools.partial(mid_kernel, (seqs, groups, cp, slots, per_expert, experts)),
        [
            ((total, width), F32),
            ((total, width), BF16),
            ((total, experts), F32),
            ((1, width), F32),
        ]
        + [((2 * per_expert, width), BF16)],
        [o_mine, x_flat.reshape(total, width), ids_flat, slot_cols, w_small],
        name="mid",
        after=cot_parts[0],
    )

    slot_parts = to_experts(send)
    dx_sent, saved = [[], []], []
    for i in range(2):
        for j in range(low):
            dx_part, *rest = call(
                functools.partial(expert_kernel, (1, cp, slots)),
                [((per_expert, width), BF16)]
                + [((per_expert, ff), BF16)] * 4
                + [((per_expert, width), BF16)],
                [slot_parts[i][j], cot_parts[i][j], up_own, down_own, up_got, down_got],
                name="expert",
            )
            dx_sent[i].append(dx_part)
            saved.append(rest)
    grad_down, grad_down_away = call(
        functools.partial(down_grad_kernel, 2 * low),
        [((width, ff), F32), ((width, ff), BF16)],
        [item for one in saved for item in (one[0], one[1], one[4])],
        name="down_grad",
    )
    grad_down_pair = lax.all_gather(grad_down_away, "hi", axis=0)
    dx_sum = []
    for i in range(2):
        dx_sum += call(
            functools.partial(add_kernel, (cp, slots)),
            [((per_expert, width), BF16)],
            from_experts(dx_sent[i]),
            name="add_dx",
            after=[grad_down_away] if i else [],
        )
    y_sent = call(
        functools.partial(expert_out_kernel, (2 * low, 1)),
        [((per_expert, width), BF16)] * (2 * low),
        [item for one in saved for item in one[:2]] + [down_own, down_got],
        name="expert_out",
        after=[dx_sum[1]],
    )
    dx_swapped = permute_xor(dx_sum[1], "dp", low)
    ret_dx = [
        swap_seq(item.reshape(seq, cp, width)).reshape(per_expert, width)
        for item in (dx_sum[0], dx_swapped)
    ]
    y_back = [from_experts(y_sent[:low]), from_experts(y_sent[low:])]

    dx1, da, do_send, dlogits, prod = call(
        functools.partial(back_kernel, (seqs, groups, cp, slots, per_expert, local)),
        [
            ((total, width), F32),
            ((total, width), BF16),
            ((seq, rows, width_h), BF16),
            ((total, experts), F32),
            ((total, width), BF16),
        ],
        ret_dx
        + [x1, probs, ids_flat, slot_cols, cot_flat, w_small, gain_second],
        name="back",
        after=[y_sent[0]],
    )
    do_all = swap_seq(do_send).reshape(length, width_h)

    small_sent = call(
        functools.partial(small_grad_kernel, (seqs, groups)),
        [((width // dp, small_cols), BF16)] * dp,
        [meta, o_mine, da, xn2, dlogits, prod],
        scratch=[pltpu.VMEM((width, small_cols), BF16)],
        smem=1,
        name="small_grad",
    )
    small_got = [permute_xor(small_sent[j], "dp", j) if j else small_sent[j] for j in range(dp)]
    y_first, y_second = call(
        functools.partial(add_both_kernel, None),
        [((per_expert, width), BF16)] * 2,
        y_back[0] + y_back[1],
        name="add_y",
        after=[small_sent[0]],
    )

    y_swapped = permute_xor(y_second, "dp", low)
    (grad_up_away,) = call(
        functools.partial(up_grad_kernel, (2 * low, 1)),
        [((width, ff), BF16)],
        sum(slot_parts, []) + [one[3] for one in saved],
        name="up_grad_away",
        after=[y_swapped],
    )
    grad_up_pair = lax.all_gather(grad_up_away, "hi", axis=0)
    (y_pair,) = call(
        functools.partial(side_kernel, None),
        [((seq, 2 * cp, width), BF16)],
        [item.reshape(seq, cp, width) for item in (y_first, y_swapped)],
        name="side",
    )
    y_got = swap_seq(y_pair).reshape(seq, 2, cp, width)
    mixed_in = [y_got[:, k].reshape(per_expert, width) for k in range(2)]
    (mixed,) = call(
        functools.partial(mixed_kernel, (per_expert, local)),
        [((total, width), BF16)],
        mixed_in + [x1, probs, ids_flat, slot_cols],
        name="mixed",
    )


    span = length + block
    dx_own, dx_sib, dqkv, table_own = call(
        functools.partial(attn_bwd_kernel, (half, hpd, block, scale, rel_bias.shape[0])),
        [
            ((half, rows, width), BF16),
            ((half, rows, width), BF16),
            ((length, cols), BF16),
            ((8, LANES), F32),
        ],
        [meta, do_all, qkv, w_mine, lse, slab, hot_rev],
        scratch=[
            pltpu.VMEM((length, HD), F32),
            pltpu.VMEM((length, HD), F32),
            pltpu.VMEM((block, span), F32),
            pltpu.VMEM((8, span), F32),
        ],
        smem=1,
        name="attn_bwd",
        after=[y_pair, grad_up_away, small_sent[0]],
    )
    pairs = call(
        functools.partial(pair_kernel, None),
        [((rows, width), BF16)] * half,
        [dx_own, permute_xor(dx_sib, "seq", 1)],
        name="pair",
    )
    dx_parts = [permute_xor(pairs[k], "seq", 2 * k) if k else pairs[k] for k in range(half)]
    (grad_tokens,) = call(
        functools.partial(last_kernel, (half, seqs, groups)),
        [((total, width), BF16)],
        [meta] + dx_parts + [x_flat.reshape(total, width), dx1, gain_first],
        scratch=[pltpu.VMEM((seqs, rows, width), F32)],
        smem=1,
        name="last",
    )

    (grad_up,) = call(
        functools.partial(up_grad_kernel, (2 * low, 1)),
        [((width, ff), F32)],
        sum(slot_parts, []) + [one[2] for one in saved],
        name="up_grad",
        after=[pairs[0]],
    )
    cols_sent = call(
        functools.partial(cols_kernel, None),
        [((width // dp + 16, cols), BF16)] * dp,
        [meta, xn1, dqkv, table_own],
        scratch=[pltpu.VMEM((width, cols), BF16)],
        smem=1,
        name="cols",
        after=[pairs[0]],
    )
    cols_got = [permute_xor(cols_sent[j], "dp", j) if j else cols_sent[j] for j in range(dp)]
    line_rows = -(-shard // 8) * 8 + 8
    (line,) = call(
        functools.partial(merge_kernel, (dp, shard)),
        [((seq, line_rows, cols + small_cols), BF16)],
        cols_got + small_got,
        scratch=[pltpu.VMEM((width // dp, cols + small_cols), F32)],
        name="merge",
        after=dx_parts[1:],
    )
    both_up, both_down = call(
        functools.partial(both_experts_kernel, None),
        [((local, width, ff), F32)] * 2,
        [meta, grad_up, grad_up_pair, grad_down, grad_down_pair],
        smem=1,
        name="both_experts",
    )
    grad_qkv, grad_out, grad_router, grad_first, grad_second, table = call(
        functools.partial(finish_kernel, (seqs, groups, hpd, cols, experts)),
        [
            ((shard, 3 * width), F32),
            ((shard, width), F32),
            ((shard, experts), F32),
            ((1, shard), F32),
            ((1, shard), F32),
            ((8, LANES), F32),
        ],
        [swap_seq(line), w_qkv, gain_attn[:, None]],
        name="finish",
        after=[grad_tokens, mixed, both_up],
    )
    table = table.reshape(8, repeat, rel_bias.shape[0])
    table = jnp.transpose(table, (2, 1, 0)).reshape(rel_bias.shape[0], 8 * repeat)
    table_grad = table[:, :heads]

    return (
        mixed.reshape(tokens.shape),
        grad_tokens.reshape(tokens.shape),
        grad_first.reshape(shard),
        grad_qkv,
        table_grad,
        grad_out,
        grad_second.reshape(shard),
        grad_router,
        both_up,
        both_down,
    )


def solution(mesh):
    dp, seq = mesh.devices.shape
    mesh = Mesh(mesh.devices.reshape(2, dp // 2, seq), DP + ("seq",))
    in_specs = (
        P(None, DP, "seq", None),
        P(None, DP, "seq", None),
        P(None, DP, "seq", None),
        P(),
        P(("hi", "lo", "seq")),
        P(("hi", "lo", "seq"), None),
        P(),
        P(("hi", "lo", "seq"), None),
        P(("hi", "lo", "seq")),
        P(("hi", "lo", "seq"), None),
        P("seq", None, DP),
        P("seq", None, DP),
    )
    out_specs = (
        P(None, DP, "seq", None),
        P(None, DP, "seq", None),
        P(("hi", "lo", "seq")),
        P(("hi", "lo", "seq"), None),
        P(),
        P(("hi", "lo", "seq"), None),
        P(("hi", "lo", "seq")),
        P(("hi", "lo", "seq"), None),
        P("seq", None, DP),
        P("seq", None, DP),
    )
    return jax.shard_map(shards, mesh=mesh, in_specs=in_specs, out_specs=out_specs, check_vma=False)
```

profile of v0, /device:TPU:0, one launch (start us, length us, event | category | flops | bytes accessed | tf_op | source)
XLA Modules:
  0.0 402.5 jit_solution(6896279245560807118)
XLA Ops:
  13.2 6.3 %all-to-all-start = ((bf16[8,24,640]{2,1,0:T(8,128)(2,1)}), bf16[8,24,640]{2,1,0:T(8,128)(2,1)S(1)}, u32[]{:S(2)}, u32[]{:S(2)}) async-start(bf16[8,24,640]{2,1,0:T(8,128)(2,1)} %bitcast.10), calls=%async_computation | async-start | bytes 491520 | tf_op jit(solution)/shard_map/all_to_all | solution.py:607
  21.6 2.4 collective-permute-start.1
  24.1 11.4 %collective-permute-done.refs_3_.refs_2_ = bf16[128,768]{1,0:T(8,128)(2,1)S(1)} collective-permute-done((bf16[128,768]{1,0:T(8,128)(2,1)S(1)}, bf16[128,768]{1,0:T(8,128)(2,1)S(1)}, u32[]{:S(2)}, u32[]{:S(2)}) %collective-permute-start) | collective-permute-done | bytes 196640 | tf_op jit(solution)/shard_map/ppermute | solution.py:599
  37.1 5.8 %collective-permute-done.1.refs_4_.refs_3_ = bf16[128,768]{1,0:T(8,128)(2,1)S(1)} collective-permute-done((bf16[128,768]{1,0:T(8,128)(2,1)S(1)}, bf16[128,768]{1,0:T(8,128)(2,1)S(1)}, u32[]{:S(2)}, u32[]{:S(2)}) %collective-permute-start.1) | collective-permute-done | bytes 196640 | tf_op jit(solution)/shard_map/ppermute | solution.py:599
  47.9 5.8 %collective-permute-done.8.refs_12_.refs_11_ = bf16[192,640]{1,0:T(8,128)(2,1)S(1)} collective-permute-done((bf16[192,640]{1,0:T(8,128)(2,1)S(1)}, bf16[192,640]{1,0:T(8,128)(2,1)S(1)}, u32[]{:S(2)}, u32[]{:S(2)}) %collective-permute-start.8) | collective-permute-done | bytes 245792 | tf_op jit(solution)/shard_map/ppermute | solution.py:599
  54.5 3.6 route.1
  58.2 5.1 %all-to-all-start.2 = ((bf16[8,80,768]{2,1,0:T(8,128)(2,1)}), bf16[8,80,768]{2,1,0:T(8,128)(2,1)S(1)}, u32[]{:S(2)}, u32[]{:S(2)}) async-start(bf16[8,80,768]{2,1,0:T(8,128)(2,1)} %bitcast.81), calls=%async_computation.2 | async-start | bytes 1966080 | tf_op jit(solution)/shard_map/all_to_all | solution.py:607
  63.5 3.7 constant_dynamic-slice_fusion
  72.6 11.7 %attn_fwd.1 = (bf16[1024,192]{1,0:T(8,128)(2,1)}, bf16[1024,640]{1,0:T(8,128)(2,1)}, bf16[1024,768]{1,0:T(8,128)(2,1)}, bf16[768,640]{1,0:T(8,128)(2,1)}, f32[10...) custom-call(s32[5]{0:T(128)} %stack.28.refs_0_, bf16[128,768]{1,0:T(8,128)(2,1)} %copy-done.18, ...), custom_call_target="tpu_custom_call" | custom-call | bytes 1 | tf_op jit(solution)/shard_map/attn_fwd/pallas_call | solution.py:55
  86.3 5.8 %all-to-all-done.2 = bf16[8,80,768]{2,1,0:T(8,128)(2,1)S(1)} async-done(((bf16[8,80,768]{2,1,0:T(8,128)(2,1)}), bf16[8,80,768]{2,1,0:T(8,128)(2,1)S(1)}, u32[]{:S(2)}, u32[]{:S(2)}) %all-to-all-start.2) | async-done | bytes 983072 | tf_op jit(solution)/shard_map/all_to_all | solution.py:607
  92.1 3.5 all-to-all-start.1
  97.2 10.8 %all-to-all-done.1 = bf16[8,128,192]{1,2,0:T(8,128)(2,1)S(1)} async-done(((bf16[8,128,192]{1,2,0:T(8,128)(2,1)}), bf16[8,128,192]{1,2,0:T(8,128)(2,1)S(1)}, u32[]{:S(2)}, u32[]{:S(2)}) %all-to-all-start.1) | async-done | bytes 393248 | tf_op jit(solution)/shard_map/all_to_all | solution.py:607
  110.1 4.7 %mid.1 = (f32[256,768]{1,0:T(8,128)}, bf16[256,768]{1,0:T(8,128)(2,1)}, f32[256,16]{1,0:T(8,128)}, f32[1,768]{1,0:T(1,128)}, bf16[640,768]{1,0:T(8,128)(2,1)}) custom-call(bf16[8,128,192]{2,1,0:T(8,128)(2,1)} %copy.50.refs_0_.refs_1_, bf16[256,768]{1,0:T(8,128)(2,1)} %bitcast.74, s32[256,2]{1,0:T(8,128)} %bitcast.84, ...), custom_call_target="tpu_custom_call" | custom-call | bytes 1 | tf_op jit(solution)/shard_map/mid/pallas_call | solution.py:55
  114.8 5.2 %all-to-all-start.3 = ((bf16[8,80,768]{2,1,0:T(8,128)(2,1)}), bf16[8,80,768]{2,1,0:T(8,128)(2,1)S(1)}, u32[]{:S(2)}, u32[]{:S(2)}) async-start(bf16[8,80,768]{2,1,0:T(8,128)(2,1)} %bitcast.107), calls=%async_computation.3 | async-start | bytes 1966080 | tf_op jit(solution)/shard_map/all_to_all | solution.py:607
  121.6 23.6 %all-to-all-done.3 = bf16[8,80,768]{2,1,0:T(8,128)(2,1)S(1)} async-done(((bf16[8,80,768]{2,1,0:T(8,128)(2,1)}), bf16[8,80,768]{2,1,0:T(8,128)(2,1)S(1)}, u32[]{:S(2)}, u32[]{:S(2)}) %all-to-all-start.3) | async-done | bytes 983072 | tf_op jit(solution)/shard_map/all_to_all | solution.py:607
  148.8 17.4 %collective-permute-done.12.refs_0_.refs_2_ = bf16[320,768]{1,0:T(8,128)(2,1)S(1)} collective-permute-done((bf16[320,768]{1,0:T(8,128)(2,1)S(1)}, bf16[320,768]{1,0:T(8,128)(2,1)S(1)}, u32[]{:S(2)}, u32[]{:S(2)}) %collective-permute-start.12) | collective-permute-done | bytes 491552 | tf_op jit(solution)/shard_map/ppermute | solution.py:599
  167.7 3.2 dynamic-slice_bitcast_fusion
  171.7 6.4 %expert.5 = (bf16[320,768]{1,0:T(8,128)(2,1)}, bf16[320,768]{1,0:T(8,128)(2,1)}, bf16[320,768]{1,0:T(8,128)(2,1)}, bf16[320,768]{1,0:T(8,128)(2,1)}, bf16[320,768]{1,0:T(8,128)(2,1)}, /*index=5*/bf16[320,768]{1,0:T(8,128)(2,1)}) custom-call(bf16[320,768]{1,0:T(8,128)(2,1)} %copy-done.6, bf16[320,768]{1,0:T(8,128)(2,1)} %copy-done.13, ...), custom_call_target="tpu_custom_call" | custom-call | bytes 1 | tf_op jit(solution)/shard_map/expert/pallas_call | solution.py:55
  181.2 6.4 %expert.7 = (bf16[320,768]{1,0:T(8,128)(2,1)}, bf16[320,768]{1,0:T(8,128)(2,1)}, bf16[320,768]{1,0:T(8,128)(2,1)}, bf16[320,768]{1,0:T(8,128)(2,1)}, bf16[320,768]{1,0:T(8,128)(2,1)}, /*index=5*/bf16[320,768]{1,0:T(8,128)(2,1)}) custom-call(bf16[320,768]{1,0:T(8,128)(2,1)} %copy-done.7, bf16[320,768]{1,0:T(8,128)(2,1)} %copy-done.35, ...), custom_call_target="tpu_custom_call" | custom-call | bytes 1 | tf_op jit(solution)/shard_map/expert/pallas_call | solution.py:55
  187.5 2.4 collective-permute-start.16
  189.9 6.4 %expert.4 = (bf16[320,768]{1,0:T(8,128)(2,1)}, bf16[320,768]{1,0:T(8,128)(2,1)}, bf16[320,768]{1,0:T(8,128)(2,1)}, bf16[320,768]{1,0:T(8,128)(2,1)}, bf16[320,768]{1,0:T(8,128)(2,1)}, /*index=5*/bf16[320,768]{1,0:T(8,128)(2,1)}) custom-call(bf16[320,768]{1,0:T(8,128)(2,1)} %bitcast.71, bf16[320,768]{1,0:T(8,128)(2,1)} %bitcast.78, ...), custom_call_target="tpu_custom_call" | custom-call | bytes 1 | tf_op jit(solution)/shard_map/expert/pallas_call | solution.py:55
  199.3 3.5 all-to-all-start.4
  203.0 6.4 %expert.6 = (bf16[320,768]{1,0:T(8,128)(2,1)}, bf16[320,768]{1,0:T(8,128)(2,1)}, bf16[320,768]{1,0:T(8,128)(2,1)}, bf16[320,768]{1,0:T(8,128)(2,1)}, bf16[320,768]{1,0:T(8,128)(2,1)}, /*index=5*/bf16[320,768]{1,0:T(8,128)(2,1)}) custom-call(bf16[320,768]{1,0:T(8,128)(2,1)} %copy-done.5, bf16[320,768]{1,0:T(8,128)(2,1)} %copy-done.34, ...), custom_call_target="tpu_custom_call" | custom-call | bytes 1 | tf_op jit(solution)/shard_map/expert/pallas_call | solution.py:55
  209.5 9.3 %down_grad.1 = (f32[768,768]{1,0:T(8,128)}, bf16[768,768]{1,0:T(8,128)(2,1)}) custom-call(bf16[320,768]{1,0:T(8,128)(2,1)} %get-tuple-element.89.refs_0_, bf16[320,768]{1,0:T(8,128)(2,1)} %get-tuple-element.90.refs_1_, bf16[320,768]{1,0:T(8,128)(2,1)} %get-tuple-element.99.refs_2_, bf16[320,768]{1,0:T(8,128)(2,1)} %get-tuple-element.91.refs_3_.refs_2_, ...), custom_call_target="tpu_custom_call" | custom-call | bytes 1 | tf_op jit(solution)/shard_map/down_grad/pallas_call | solution.py:55
  222.4 15.6 %collective-permute-done.20 = bf16[320,768]{1,0:T(8,128)(2,1)} collective-permute-done((bf16[320,768]{1,0:T(8,128)(2,1)}, bf16[320,768]{1,0:T(8,128)(2,1)}, u32[]{:S(2)}, u32[]{:S(2)}) %collective-permute-start.20) | collective-permute-done | bytes 491552 | tf_op jit(solution)/shard_map/ppermute | solution.py:599
  238.0 5.2 %all-to-all-start.5 = ((bf16[8,40,768]{2,1,0:T(8,128)(2,1)}), bf16[8,40,768]{2,1,0:T(8,128)(2,1)S(1)}, u32[]{:S(2)}, u32[]{:S(2)}) async-start(bf16[8,40,768]{2,1,0:T(8,128)(2,1)} %bitcast.33), calls=%async_computation.5 | async-start | bytes 983040 | tf_op jit(solution)/shard_map/all_to_all | solution.py:607
  243.2 6.8 %expert_out.1 = (bf16[320,768]{1,0:T(8,128)(2,1)}, bf16[320,768]{1,0:T(8,128)(2,1)}, bf16[320,768]{1,0:T(8,128)(2,1)}, bf16[320,768]{1,0:T(8,128)(2,1)}) custom-call(bf16[320,768]{1,0:T(8,128)(2,1)} %get-tuple-element.89.refs_0_, bf16[320,768]{1,0:T(8,128)(2,1)} %get-tuple-element.90.refs_1_, bf16[320,768]{1,0:T(8,128)(2,1)} %get-tuple-element.91.refs_3_.refs_2_, ...), custom_call_target="tpu_custom_call" | custom-call | bytes 1 | tf_op jit(solution)/shard_map/expert_out/pallas_call | solution.py:55
  252.1 5.8 %all-to-all-done.5 = bf16[8,40,768]{2,1,0:T(8,128)(2,1)S(1)} async-done(((bf16[8,40,768]{2,1,0:T(8,128)(2,1)}), bf16[8,40,768]{2,1,0:T(8,128)(2,1)S(1)}, u32[]{:S(2)}, u32[]{:S(2)}) %all-to-all-start.5) | async-done | bytes 491552 | tf_op jit(solution)/shard_map/all_to_all | solution.py:607
  258.7 5.1 %back.1 = (f32[256,768]{1,0:T(8,128)}, bf16[256,768]{1,0:T(8,128)(2,1)}, bf16[8,128,192]{2,1,0:T(8,128)(2,1)}, f32[256,16]{1,0:T(8,128)}, bf16[256,768]{1,0:T(8,128)(2,1)}) custom-call(bf16[320,768]{1,0:T(8,128)(2,1)} %bitcast.97, bf16[320,768]{1,0:T(8,128)(2,1)} %bitcast.99, f32[256,768]{1,0:T(8,128)} %get-tuple-element.110.refs_2_, ...), custom_call_target="tpu_custom_call" | custom-call | bytes 1 | tf_op jit(solution)/shard_map/back/pallas_call | solution.py:55
  265.8 3.5 all-to-all-start.7
  269.2 3.8 small_grad.1
  275.2 2.6 add_y.1
  278.3 12.5 %collective-permute-done.21.refs_8_ = bf16[320,768]{1,0:T(8,128)(2,1)S(1)} collective-permute-done((bf16[320,768]{1,0:T(8,128)(2,1)}, bf16[320,768]{1,0:T(8,128)(2,1)S(1)}, u32[]{:S(2)}, u32[]{:S(2)}) %collective-permute-start.21) | collective-permute-done | bytes 491552 | tf_op jit(solution)/shard_map/ppermute | solution.py:599
  293.8 4.3 %all-to-all-start.6 = ((bf16[8,80,768]{2,1,0:T(8,128)(2,1)}), bf16[8,80,768]{2,1,0:T(8,128)(2,1)S(1)}, u32[]{:S(2)}, u32[]{:S(2)}) async-start(bf16[8,80,768]{2,1,0:T(8,128)(2,1)} %side.1.refs_7_), calls=%async_computation.6 | async-start | bytes 1966080 | tf_op jit(solution)/shard_map/all_to_all | solution.py:607
  298.4 5.8 %up_grad_away.1.refs_8_ = bf16[768,768]{1,0:T(8,128)(2,1)} custom-call(bf16[320,768]{1,0:T(8,128)(2,1)} %bitcast.72, bf16[320,768]{1,0:T(8,128)(2,1)} %copy-done.6, bf16[320,768]{1,0:T(8,128)(2,1)} %copy-done.5, bf16[320,768]{1,0:T(8,128)(2,1)} %copy-done.7, bf16[320,768]{1,0:T(8,128)(2,1)} %get-tuple-element.125.refs_4_, ...), custom_call_target="tpu_custom_call" | custom-call | bytes 1 | tf_op jit(solution)/shard_map/up_grad_away/pallas_call | solution.py:55
  305.2 16.6 %attn_bwd.1 = (bf16[4,128,768]{2,1,0:T(8,128)(2,1)}, bf16[4,128,768]{2,1,0:T(8,128)(2,1)}, bf16[1024,640]{1,0:T(8,128)(2,1)}, f32[8,128]{1,0:T(8,128)}) custom-call(s32[5]{0:T(128)} %stack.28.refs_0_, bf16[1024,192]{1,0:T(8,128)(2,1)} %bitcast.94, bf16[1024,640]{1,0:T(8,128)(2,1)} %get-tuple-element.121.refs_2_, ...), custom_call_target="tpu_custom_call" | custom-call | bytes 1 | tf_op jit(solution)/shard_map/attn_bwd/pallas_call | solution.py:55
  323.5 2.3 collective-permute-start.31
  326.7 2.4 pair.1
  330.8 4.5 %cols.1 = (bf16[208,640]{1,0:T(8,128)(2,1)}, bf16[208,640]{1,0:T(8,128)(2,1)}, bf16[208,640]{1,0:T(8,128)(2,1)}, bf16[208,640]{1,0:T(8,128)(2,1)}) custom-call(s32[5]{0:T(128)} %stack.28.refs_0_, bf16[1024,768]{1,0:T(8,128)(2,1)} %get-tuple-element.137.refs_1_, bf16[1024,640]{1,0:T(8,128)(2,1)} %get-tuple-element.138.refs_2_, ...), custom_call_target="tpu_custom_call" | custom-call | bytes 1 | tf_op jit(solution)/shard_map/cols/pallas_call | solution.py:55
  336.4 5.6 %collective-permute-done.30.refs_6_ = bf16[192,896]{1,0:T(8,128)(2,1)S(1)} collective-permute-done((bf16[192,896]{1,0:T(8,128)(2,1)S(1)}, bf16[192,896]{1,0:T(8,128)(2,1)S(1)}, u32[]{:S(2)}, u32[]{:S(2)}) %collective-permute-start.30) | collective-permute-done | bytes 344096 | tf_op jit(solution)/shard_map/ppermute | solution.py:599
  343.8 2.8 collective-permute-start.24
  348.1 8.9 %collective-permute-done.24.refs_3_.refs_9_ = bf16[128,768]{1,0:T(8,128)(2,1)S(1)} collective-permute-done((bf16[128,768]{1,0:T(8,128)(2,1)S(1)}, bf16[128,768]{1,0:T(8,128)(2,1)S(1)}, u32[]{:S(2)}, u32[]{:S(2)}) %collective-permute-start.24) | collective-permute-done | bytes 196640 | tf_op jit(solution)/shard_map/ppermute | solution.py:599
  359.4 2.8 merge.1
  362.1 5.5 %all-to-all-start.8 = ((bf16[8,32,1536]{2,1,0:T(8,128)(2,1)}), bf16[8,32,1536]{2,1,0:T(8,128)(2,1)S(1)}, u32[]{:S(2)}, u32[]{:S(2)}) async-start(bf16[8,32,1536]{2,1,0:T(8,128)(2,1)} %merge.1), calls=%async_computation.8 | async-start | bytes 1572864 | tf_op jit(solution)/shard_map/all_to_all | solution.py:607
  368.3 6.2 %up_grad.1.refs_1_ = f32[768,768]{1,0:T(8,128)} custom-call(bf16[320,768]{1,0:T(8,128)(2,1)} %bitcast.73, bf16[320,768]{1,0:T(8,128)(2,1)} %copy-done.6, bf16[320,768]{1,0:T(8,128)(2,1)} %copy-done.5, bf16[320,768]{1,0:T(8,128)(2,1)} %copy-done.7, bf16[320,768]{1,0:T(8,128)(2,1)} %get-tuple-element.147.refs_4_, bf16[320,768]{1,0:T(8,128)(2,1)} %get-tuple-element.148.refs_5_, ...), custom_call_target="tpu_custom_call" | custom-call | bytes 1 | tf_op jit(solution)/shard_map/up_grad/pallas_call | solution.py:55
  374.5 2.8 last.1.refs_3_
  378.4 3.3 mixed.1.refs_4_
  381.7 8.0 %both_experts.1 = (f32[2,768,768]{2,1,0:T(8,128)}, f32[2,768,768]{2,1,0:T(8,128)}) custom-call(s32[5]{0:T(128)} %stack.28.refs_0_, f32[768,768]{1,0:T(8,128)} %up_grad.1.refs_1_, bf16[2,768,768]{2,1,0:T(8,128)(2,1)} %bitcast.88, f32[768,768]{1,0:T(8,128)} %get-tuple-element.151.refs_3_, bf16[2,768,768]{2,1,0:T(8,128)(2,1)} %bitcast.87), custom_call_target="tpu_custom_call" | custom-call | bytes 1 | tf_op jit(solution)/shard_map/both_experts/pallas_call | solution.py:55
  (206 shorter events, 74.3 us)
Async XLA Ops:
  7.2 61.7 %copy-start = (bf16[32,12]{0,1:T(8,128)(2,1)S(1)}, bf16[32,12]{0,1:T(8,128)(2,1)}, u32[]{:S(2)}) copy-start(bf16[32,12]{0,1:T(8,128)(2,1)} %param.18) | copy-start | bytes 2308
  7.2 101.9 %all-gather.8.cloned.1.call-start = ((), (), s32[]{:S(2)}) async-start(), calls=%async_computation.9 | async-start | bytes 1419264 | tf_op jit(solution)/shard_map/all_gather | solution.py:674
  12.4 34.0 %copy-start.43 = (s32[2,1,128,2]{2,3,1,0:T(2,128)S(1)}, s32[2,1,128,2]{2,3,1,0:T(2,128)}, u32[]{:S(2)}) copy-start(s32[2,1,128,2]{2,3,1,0:T(2,128)} %param.14) | copy-start | bytes 6148
  13.2 22.4 %all-to-all-start = ((bf16[8,24,640]{2,1,0:T(8,128)(2,1)}), bf16[8,24,640]{2,1,0:T(8,128)(2,1)S(1)}, u32[]{:S(2)}, u32[]{:S(2)}) async-start(bf16[8,24,640]{2,1,0:T(8,128)(2,1)} %bitcast.10), calls=%async_computation | async-start | bytes 491520 | tf_op jit(solution)/shard_map/all_to_all | solution.py:607
  19.6 38.6 %copy-start.18 = (bf16[128,768]{1,0:T(8,128)(2,1)}, bf16[128,768]{1,0:T(8,128)(2,1)S(1)}, u32[]{:S(2)}) copy-start(bf16[128,768]{1,0:T(8,128)(2,1)S(1)} %get-tuple-element.205.refs_1_) | copy-start | bytes 589828
  19.6 15.9 %collective-permute-start = (bf16[128,768]{1,0:T(8,128)(2,1)S(1)}, bf16[128,768]{1,0:T(8,128)(2,1)S(1)}, u32[]{:S(2)}, u32[]{:S(2)}) collective-permute-start(bf16[128,768]{1,0:T(8,128)(2,1)S(1)} %get-tuple-element.204), channel_id=1, source_target_pairs={{0,2},{1,3},{2,0},{3,1},{4,6},{5,7},{6,4},{7,5},{8,10},{9,11},{10,... | collective-permute-start | bytes 589832 | tf_op jit(solution)/shard_map/ppermute | solution.py:599
  21.6 21.3 %collective-permute-start.1 = (bf16[128,768]{1,0:T(8,128)(2,1)S(1)}, bf16[128,768]{1,0:T(8,128)(2,1)S(1)}, u32[]{:S(2)}, u32[]{:S(2)}) collective-permute-start(bf16[128,768]{1,0:T(8,128)(2,1)S(1)} %get-tuple-element.203), channel_id=1, source_target_pairs={{0,4},{1,5},{2,6},{3,7},{4,0},{5,1},{6,2},{7,3},{8,12},{9,13},{10,... | collective-permute-start | bytes 589832 | tf_op jit(solution)/shard_map/ppermute | solution.py:599
  24.0 20.4 %collective-permute-start.2 = (bf16[128,768]{1,0:T(8,128)(2,1)S(1)}, bf16[128,768]{1,0:T(8,128)(2,1)S(1)}, u32[]{:S(2)}, u32[]{:S(2)}) collective-permute-start(bf16[128,768]{1,0:T(8,128)(2,1)S(1)} %get-tuple-element.202), channel_id=1, source_target_pairs={{0,6},{1,7},{2,4},{3,5},{4,2},{5,3},{6,0},{7,1},{8,14},{9,15},{10,... | collective-permute-start | bytes 589832 | tf_op jit(solution)/shard_map/ppermute | solution.py:599
  24.1 21.8 %collective-permute-start.3 = (bf16[128,768]{1,0:T(8,128)(2,1)S(1)}, bf16[128,768]{1,0:T(8,128)(2,1)S(1)}, u32[]{:S(2)}, u32[]{:S(2)}) collective-permute-start(bf16[128,768]{1,0:T(8,128)(2,1)S(1)} %get-tuple-element.205.refs_1_), channel_id=1, source_target_pairs={{0,1},{1,0},{2,3},{3,2},{4,5},{5,4},{6,7},{7,6},{8,9},{9,8},{10,11... | collective-permute-start | bytes 589832 | tf_op jit(solution)/shard_map/ppermute | solution.py:599
  35.5 10.4 %collective-permute-start.4 = (bf16[128,768]{1,0:T(8,128)(2,1)S(1)}, bf16[128,768]{1,0:T(8,128)(2,1)S(1)}, u32[]{:S(2)}, u32[]{:S(2)}) collective-permute-start(bf16[128,768]{1,0:T(8,128)(2,1)S(1)} %collective-permute-done.refs_3_.refs_2_), channel_id=1, source_target_pairs={{0,1},{1,0},{2,3},{3,2},{4,5},{5,4},{6,7},{7,6},{8,9},{9,8},{10,11... | collective-permute-start | bytes 589832 | tf_op jit(solution)/shard_map/ppermute | solution.py:599
  35.5 12.3 %collective-permute-start.7 = (bf16[192,640]{1,0:T(8,128)(2,1)S(1)}, bf16[192,640]{1,0:T(8,128)(2,1)S(1)}, u32[]{:S(2)}, u32[]{:S(2)}) collective-permute-start(bf16[192,640]{1,0:T(8,128)(2,1)S(1)} %bitcast.89), channel_id=1, source_target_pairs={{0,8},{8,0},{16,24},{24,16},{1,9},{9,1},{17,25},{25,17},{2,10},{10... | collective-permute-start | bytes 737288 | tf_op jit(solution)/shard_map/ppermute | solution.py:599
  42.9 10.8 %collective-permute-start.8 = (bf16[192,640]{1,0:T(8,128)(2,1)S(1)}, bf16[192,640]{1,0:T(8,128)(2,1)S(1)}, u32[]{:S(2)}, u32[]{:S(2)}) collective-permute-start(bf16[192,640]{1,0:T(8,128)(2,1)S(1)} %bitcast.90), channel_id=1, source_target_pairs={{0,16},{8,24},{16,0},{24,8},{1,17},{9,25},{17,1},{25,9},{2,18},{10... | collective-permute-start | bytes 737288 | tf_op jit(solution)/shard_map/ppermute | solution.py:599
  44.4 9.3 %collective-permute-start.9 = (bf16[192,640]{1,0:T(8,128)(2,1)S(1)}, bf16[192,640]{1,0:T(8,128)(2,1)S(1)}, u32[]{:S(2)}, u32[]{:S(2)}) collective-permute-start(bf16[192,640]{1,0:T(8,128)(2,1)S(1)} %bitcast.91), channel_id=1, source_target_pairs={{0,24},{8,16},{16,8},{24,0},{1,25},{9,17},{17,9},{25,1},{2,26},{10... | collective-permute-start | bytes 737288 | tf_op jit(solution)/shard_map/ppermute | solution.py:599
  45.9 2.0 collective-permute-start.5
  45.9 2.0 collective-permute-start.6
  58.2 33.9 %all-to-all-start.2 = ((bf16[8,80,768]{2,1,0:T(8,128)(2,1)}), bf16[8,80,768]{2,1,0:T(8,128)(2,1)S(1)}, u32[]{:S(2)}, u32[]{:S(2)}) async-start(bf16[8,80,768]{2,1,0:T(8,128)(2,1)} %bitcast.81), calls=%async_computation.2 | async-start | bytes 1966080 | tf_op jit(solution)/shard_map/all_to_all | solution.py:607
  63.2 104.5 %all-gather.10.cloned.1.call-start = ((), (), s32[]{:S(2)}) async-start(), calls=%async_computation.10 | async-start | bytes 7077888 | tf_op jit(solution)/shard_map/all_gather | solution.py:716
  92.1 15.9 %all-to-all-start.1 = ((bf16[8,128,192]{1,2,0:T(8,128)(2,1)}), bf16[8,128,192]{1,2,0:T(8,128)(2,1)S(1)}, u32[]{:S(2)}, u32[]{:S(2)}) async-start(bf16[8,128,192]{1,2,0:T(8,128)(2,1)} %copy.47), calls=%async_computation.1 | async-start | bytes 786432 | tf_op jit(solution)/shard_map/all_to_all | solution.py:607
  95.7 13.6 %collective-permute-start.10 = (bf16[320,768]{1,0:T(8,128)(2,1)S(1)}, bf16[320,768]{1,0:T(8,128)(2,1)S(1)}, u32[]{:S(2)}, u32[]{:S(2)}) collective-permute-start(bf16[320,768]{1,0:T(8,128)(2,1)S(1)} %bitcast.76), channel_id=1, source_target_pairs={{0,8},{8,0},{16,24},{24,16},{1,9},{9,1},{17,25},{25,17},{2,10},{10... | collective-permute-start | bytes 1474568 | tf_op jit(solution)/shard_map/ppermute | solution.py:599
  114.8 30.3 %all-to-all-start.3 = ((bf16[8,80,768]{2,1,0:T(8,128)(2,1)}), bf16[8,80,768]{2,1,0:T(8,128)(2,1)S(1)}, u32[]{:S(2)}, u32[]{:S(2)}) async-start(bf16[8,80,768]{2,1,0:T(8,128)(2,1)} %bitcast.107), calls=%async_computation.3 | async-start | bytes 1966080 | tf_op jit(solution)/shard_map/all_to_all | solution.py:607
  120.0 28.3 %collective-permute-start.13 = (bf16[320,768]{1,0:T(8,128)(2,1)S(1)}, bf16[320,768]{1,0:T(8,128)(2,1)S(1)}, u32[]{:S(2)}, u32[]{:S(2)}) collective-permute-start(bf16[320,768]{1,0:T(8,128)(2,1)S(1)} %bitcast.110), channel_id=1, source_target_pairs={{0,16},{8,24},{16,0},{24,8},{1,17},{9,25},{17,1},{25,9},{2,18},{10... | collective-permute-start | bytes 1474568 | tf_op jit(solution)/shard_map/ppermute | solution.py:599
  145.2 21.0 %collective-permute-start.12 = (bf16[320,768]{1,0:T(8,128)(2,1)S(1)}, bf16[320,768]{1,0:T(8,128)(2,1)S(1)}, u32[]{:S(2)}, u32[]{:S(2)}) collective-permute-start(bf16[320,768]{1,0:T(8,128)(2,1)S(1)} %bitcast.111), channel_id=1, source_target_pairs={{0,16},{8,24},{16,0},{24,8},{1,17},{9,25},{17,1},{25,9},{2,18},{10... | collective-permute-start | bytes 1474568 | tf_op jit(solution)/shard_map/ppermute | solution.py:599
  146.8 24.2 %collective-permute-start.11 = (bf16[320,768]{1,0:T(8,128)(2,1)S(1)}, bf16[320,768]{1,0:T(8,128)(2,1)S(1)}, u32[]{:S(2)}, u32[]{:S(2)}) collective-permute-start(bf16[320,768]{1,0:T(8,128)(2,1)S(1)} %bitcast.70), channel_id=1, source_target_pairs={{0,8},{8,0},{16,24},{24,16},{1,9},{9,1},{17,25},{25,17},{2,10},{10... | collective-permute-start | bytes 1474568 | tf_op jit(solution)/shard_map/ppermute | solution.py:599
  148.3 30.4 %collective-permute-start.15 = (bf16[320,768]{1,0:T(8,128)(2,1)S(1)}, bf16[320,768]{1,0:T(8,128)(2,1)S(1)}, u32[]{:S(2)}, u32[]{:S(2)}) collective-permute-start(bf16[320,768]{1,0:T(8,128)(2,1)S(1)} %collective-permute-done.13.refs_1_), channel_id=1, source_target_pairs={{0,8},{8,0},{16,24},{24,16},{1,9},{9,1},{17,25},{25,17},{2,10},{10... | collective-permute-start | bytes 1474568 | tf_op jit(solution)/shard_map/ppermute | solution.py:599
  166.3 14.1 %collective-permute-start.14 = (bf16[320,768]{1,0:T(8,128)(2,1)S(1)}, bf16[320,768]{1,0:T(8,128)(2,1)S(1)}, u32[]{:S(2)}, u32[]{:S(2)}) collective-permute-start(bf16[320,768]{1,0:T(8,128)(2,1)S(1)} %collective-permute-done.12.refs_0_.refs_2_), channel_id=1, source_target_pairs={{0,8},{8,0},{16,24},{24,16},{1,9},{9,1},{17,25},{25,17},{2,10},{10... | collective-permute-start | bytes 1474568 | tf_op jit(solution)/shard_map/ppermute | solution.py:599
  178.1 18.2 %collective-permute-start.19 = (bf16[320,768]{1,0:T(8,128)(2,1)}, bf16[320,768]{1,0:T(8,128)(2,1)S(1)}, u32[]{:S(2)}, u32[]{:S(2)}) collective-permute-start(bf16[320,768]{1,0:T(8,128)(2,1)} %get-tuple-element.109), channel_id=1, source_target_pairs={{0,8},{8,0},{16,24},{24,16},{1,9},{9,1},{17,25},{25,17},{2,10},{10... | collective-permute-start | bytes 1474568 | tf_op jit(solution)/shard_map/ppermute | solution.py:599
  187.5 31.2 %collective-permute-start.16 = (bf16[320,768]{1,0:T(8,128)(2,1)}, bf16[320,768]{1,0:T(8,128)(2,1)S(1)}, u32[]{:S(2)}, u32[]{:S(2)}) collective-permute-start(bf16[320,768]{1,0:T(8,128)(2,1)} %get-tuple-element.98), channel_id=1, source_target_pairs={{0,8},{8,0},{16,24},{24,16},{1,9},{9,1},{17,25},{25,17},{2,10},{10... | collective-permute-start | bytes 1474568 | tf_op jit(solution)/shard_map/ppermute | solution.py:599
  199.3 23.0 %all-to-all-start.4 = ((bf16[8,40,768]{2,1,0:T(8,128)(2,1)}), bf16[8,40,768]{2,1,0:T(8,128)(2,1)S(1)}, u32[]{:S(2)}, u32[]{:S(2)}) async-start(bf16[8,40,768]{2,1,0:T(8,128)(2,1)} %bitcast.98), calls=%async_computation.4 | async-start | bytes 983040 | tf_op jit(solution)/shard_map/all_to_all | solution.py:607
  202.8 178.8 %all-gather.14.cloned.1.call-start = ((), (), s32[]{:S(2)}) async-start(), calls=%async_computation.12 | async-start | bytes 3538944 | tf_op jit(solution)/shard_map/all_gather | solution.py:777
  221.8 16.3 %collective-permute-start.20 = (bf16[320,768]{1,0:T(8,128)(2,1)}, bf16[320,768]{1,0:T(8,128)(2,1)}, u32[]{:S(2)}, u32[]{:S(2)}) collective-permute-start(bf16[320,768]{1,0:T(8,128)(2,1)} %add_dx.2.refs_10_), channel_id=1, source_target_pairs={{0,16},{8,24},{16,0},{24,8},{1,17},{9,25},{17,1},{25,9},{2,18},{10... | collective-permute-start | bytes 1474568 | tf_op jit(solution)/shard_map/ppermute | solution.py:599
  238.0 19.8 %all-to-all-start.5 = ((bf16[8,40,768]{2,1,0:T(8,128)(2,1)}), bf16[8,40,768]{2,1,0:T(8,128)(2,1)S(1)}, u32[]{:S(2)}, u32[]{:S(2)}) async-start(bf16[8,40,768]{2,1,0:T(8,128)(2,1)} %bitcast.33), calls=%async_computation.5 | async-start | bytes 983040 | tf_op jit(solution)/shard_map/all_to_all | solution.py:607
  250.0 23.0 %collective-permute-start.17 = (bf16[320,768]{1,0:T(8,128)(2,1)}, bf16[320,768]{1,0:T(8,128)(2,1)S(1)}, u32[]{:S(2)}, u32[]{:S(2)}) collective-permute-start(bf16[320,768]{1,0:T(8,128)(2,1)} %get-tuple-element.105), channel_id=1, source_target_pairs={{0,8},{8,0},{16,24},{24,16},{1,9},{9,1},{17,25},{25,17},{2,10},{10... | collective-permute-start | bytes 1474568 | tf_op jit(solution)/shard_map/ppermute | solution.py:599
  250.0 24.4 %collective-permute-start.18 = (bf16[320,768]{1,0:T(8,128)(2,1)}, bf16[320,768]{1,0:T(8,128)(2,1)S(1)}, u32[]{:S(2)}, u32[]{:S(2)}) collective-permute-start(bf16[320,768]{1,0:T(8,128)(2,1)} %get-tuple-element.107), channel_id=1, source_target_pairs={{0,8},{8,0},{16,24},{24,16},{1,9},{9,1},{17,25},{25,17},{2,10},{10... | collective-permute-start | bytes 1474568 | tf_op jit(solution)/shard_map/ppermute | solution.py:599
  265.8 28.0 %all-to-all-start.7 = ((bf16[8,128,192]{1,2,0:T(8,128)(2,1)}), bf16[8,128,192]{1,2,0:T(8,128)(2,1)S(1)}, u32[]{:S(2)}, u32[]{:S(2)}) async-start(bf16[8,128,192]{1,2,0:T(8,128)(2,1)} %copy.54), calls=%async_computation.7 | async-start | bytes 786432 | tf_op jit(solution)/shard_map/all_to_all | solution.py:607
  277.7 13.1 %collective-permute-start.21 = (bf16[320,768]{1,0:T(8,128)(2,1)}, bf16[320,768]{1,0:T(8,128)(2,1)S(1)}, u32[]{:S(2)}, u32[]{:S(2)}) collective-permute-start(bf16[320,768]{1,0:T(8,128)(2,1)} %get-tuple-element.119), channel_id=1, source_target_pairs={{0,16},{8,24},{16,0},{24,8},{1,17},{9,25},{17,1},{25,9},{2,18},{10... | collective-permute-start | bytes 1474568 | tf_op jit(solution)/shard_map/ppermute | solution.py:599
  293.8 68.4 %all-to-all-start.6 = ((bf16[8,80,768]{2,1,0:T(8,128)(2,1)}), bf16[8,80,768]{2,1,0:T(8,128)(2,1)S(1)}, u32[]{:S(2)}, u32[]{:S(2)}) async-start(bf16[8,80,768]{2,1,0:T(8,128)(2,1)} %side.1.refs_7_), calls=%async_computation.6 | async-start | bytes 1966080 | tf_op jit(solution)/shard_map/all_to_all | solution.py:607
  298.1 83.6 %all-gather.12.cloned.1.call-start = ((), (), s32[]{:S(2)}) async-start(), calls=%async_computation.11 | async-start | bytes 3538944 | tf_op jit(solution)/shard_map/all_gather | solution.py:842
  321.7 4.1 %collective-permute-start.22 = (bf16[4,128,768]{2,1,0:T(8,128)(2,1)}, bf16[4,128,768]{2,1,0:T(8,128)(2,1)S(1)}, u32[]{:S(2)}, u32[]{:S(2)}) collective-permute-start(bf16[4,128,768]{2,1,0:T(8,128)(2,1)} %get-tuple-element.130), channel_id=1, source_target_pairs={{0,1},{1,0},{2,3},{3,2},{4,5},{5,4},{6,7},{7,6},{8,9},{9,8},{10,11... | collective-permute-start | bytes 2359304 | tf_op jit(solution)/shard_map/ppermute | solution.py:599
  322.2 13.5 %collective-permute-start.29 = (bf16[192,896]{1,0:T(8,128)(2,1)S(1)}, bf16[192,896]{1,0:T(8,128)(2,1)S(1)}, u32[]{:S(2)}, u32[]{:S(2)}) collective-permute-start(bf16[192,896]{1,0:T(8,128)(2,1)S(1)} %copy-done.47), channel_id=1, source_target_pairs={{0,8},{8,0},{16,24},{24,16},{1,9},{9,1},{17,25},{25,17},{2,10},{10... | collective-permute-start | bytes 1032200 | tf_op jit(solution)/shard_map/ppermute | solution.py:599
  322.9 19.1 %collective-permute-start.30 = (bf16[192,896]{1,0:T(8,128)(2,1)S(1)}, bf16[192,896]{1,0:T(8,128)(2,1)S(1)}, u32[]{:S(2)}, u32[]{:S(2)}) collective-permute-start(bf16[192,896]{1,0:T(8,128)(2,1)S(1)} %copy-done.46), channel_id=1, source_target_pairs={{0,16},{8,24},{16,0},{24,8},{1,17},{9,25},{17,1},{25,9},{2,18},{10... | collective-permute-start | bytes 1032200 | tf_op jit(solution)/shard_map/ppermute | solution.py:599
  323.5 20.3 %collective-permute-start.31 = (bf16[192,896]{1,0:T(8,128)(2,1)S(1)}, bf16[192,896]{1,0:T(8,128)(2,1)S(1)}, u32[]{:S(2)}, u32[]{:S(2)}) collective-permute-start(bf16[192,896]{1,0:T(8,128)(2,1)S(1)} %copy-done.45), channel_id=1, source_target_pairs={{0,24},{8,16},{16,8},{24,0},{1,25},{9,17},{17,9},{25,1},{2,26},{10... | collective-permute-start | bytes 1032200 | tf_op jit(solution)/shard_map/ppermute | solution.py:599
  329.1 17.5 %collective-permute-start.23 = (bf16[128,768]{1,0:T(8,128)(2,1)}, bf16[128,768]{1,0:T(8,128)(2,1)S(1)}, u32[]{:S(2)}, u32[]{:S(2)}) collective-permute-start(bf16[128,768]{1,0:T(8,128)(2,1)} %get-tuple-element.132), channel_id=1, source_target_pairs={{0,2},{1,3},{2,0},{3,1},{4,6},{5,7},{6,4},{7,5},{8,10},{9,11},{10,... | collective-permute-start | bytes 589832 | tf_op jit(solution)/shard_map/ppermute | solution.py:599
  335.2 21.8 %collective-permute-start.26 = (bf16[208,640]{1,0:T(8,128)(2,1)}, bf16[208,640]{1,0:T(8,128)(2,1)S(1)}, u32[]{:S(2)}, u32[]{:S(2)}) collective-permute-start(bf16[208,640]{1,0:T(8,128)(2,1)} %get-tuple-element.141), channel_id=1, source_target_pairs={{0,8},{8,0},{16,24},{24,16},{1,9},{9,1},{17,25},{25,17},{2,10},{10... | collective-permute-start | bytes 798728 | tf_op jit(solution)/shard_map/ppermute | solution.py:599
  335.7 22.9 %collective-permute-start.27 = (bf16[208,640]{1,0:T(8,128)(2,1)}, bf16[208,640]{1,0:T(8,128)(2,1)S(1)}, u32[]{:S(2)}, u32[]{:S(2)}) collective-permute-start(bf16[208,640]{1,0:T(8,128)(2,1)} %get-tuple-element.142), channel_id=1, source_target_pairs={{0,16},{8,24},{16,0},{24,8},{1,17},{9,25},{17,1},{25,9},{2,18},{10... | collective-permute-start | bytes 798728 | tf_op jit(solution)/shard_map/ppermute | solution.py:599
  342.0 16.6 %collective-permute-start.28 = (bf16[208,640]{1,0:T(8,128)(2,1)}, bf16[208,640]{1,0:T(8,128)(2,1)S(1)}, u32[]{:S(2)}, u32[]{:S(2)}) collective-permute-start(bf16[208,640]{1,0:T(8,128)(2,1)} %get-tuple-element.143), channel_id=1, source_target_pairs={{0,24},{8,16},{16,8},{24,0},{1,25},{9,17},{17,9},{25,1},{2,26},{10... | collective-permute-start | bytes 798728 | tf_op jit(solution)/shard_map/ppermute | solution.py:599
  343.8 13.3 %collective-permute-start.24 = (bf16[128,768]{1,0:T(8,128)(2,1)S(1)}, bf16[128,768]{1,0:T(8,128)(2,1)S(1)}, u32[]{:S(2)}, u32[]{:S(2)}) collective-permute-start(bf16[128,768]{1,0:T(8,128)(2,1)S(1)} %copy-done.49), channel_id=1, source_target_pairs={{0,4},{1,5},{2,6},{3,7},{4,0},{5,1},{6,2},{7,3},{8,12},{9,13},{10,... | collective-permute-start | bytes 589832 | tf_op jit(solution)/shard_map/ppermute | solution.py:599
  346.6 10.4 %collective-permute-start.25 = (bf16[128,768]{1,0:T(8,128)(2,1)S(1)}, bf16[128,768]{1,0:T(8,128)(2,1)S(1)}, u32[]{:S(2)}, u32[]{:S(2)}) collective-permute-start(bf16[128,768]{1,0:T(8,128)(2,1)S(1)} %copy-done.48), channel_id=1, source_target_pairs={{0,6},{1,7},{2,4},{3,5},{4,2},{5,3},{6,0},{7,1},{8,14},{9,15},{10,... | collective-permute-start | bytes 589832 | tf_op jit(solution)/shard_map/ppermute | solution.py:599
  362.1 27.6 %all-to-all-start.8 = ((bf16[8,32,1536]{2,1,0:T(8,128)(2,1)}), bf16[8,32,1536]{2,1,0:T(8,128)(2,1)S(1)}, u32[]{:S(2)}, u32[]{:S(2)}) async-start(bf16[8,32,1536]{2,1,0:T(8,128)(2,1)} %merge.1), calls=%async_computation.8 | async-start | bytes 1572864 | tf_op jit(solution)/shard_map/all_to_all | solution.py:607
  (47 other events, 385.4 us)
Sparse Core Ops, SparseCore 0:
  11.5 69.2 all-gather.7
  82.8 81.0 all-gather.9
  222.5 38.4 all-gather.13
  322.3 54.5 all-gather.11
where the time goes:
time: 408 us; the launch traced here: 402 us
  waiting for transfers between devices  134 us (33%)
  Pallas kernels  134 us (33%)
  starting transfers between devices  79.5 us (19%)
  local copies, waits for them, and re-layouts  36.6 us (9%)
  between operations  14.7 us (4%)
    pallas_call x25, Pallas kernels, call(): pl.pallas_call(body, out_shape=[jax.ShapeDtypeStruct(s, d) for s, d in ou...  134 us
    ppermute x32, waiting for transfers between devices, permute_xor(): return lax.ppermute(value, axis, [(i, i ^ offset) for i in range(count)])  87.9 us
    all_to_all x9, waiting for transfers between devices, swap_seq(): return lax.all_to_all(value, 'seq', split_axis=0, concat_axis=0, tiled=True)  46 us
    all_to_all x9, starting transfers between devices, swap_seq(): return lax.all_to_all(value, 'seq', split_axis=0, concat_axis=0, tiled=True)  42 us
    ppermute x32, starting transfers between devices, permute_xor(): return lax.ppermute(value, axis, [(i, i ^ offset) for i in range(count)])  36.8 us
    unnamed x103, local copies, waits for them, and re-layouts  13.2 us
  transfers between devices with their start and end apart: 45, of which 16 were waited for; matrix products, arithmetic and copies ran while one was open for 6% of the time, Pallas kernels for 33%

commit v1 on v0

--- a/solution.py
+++ b/solution.py
@@ -768,13 +768,6 @@
             )
             dx_sent[i].append(dx_part)
             saved.append(rest)
-    grad_down, grad_down_away = call(
-        functools.partial(down_grad_kernel, 2 * low),
-        [((width, ff), F32), ((width, ff), BF16)],
-        [item for one in saved for item in (one[0], one[1], one[4])],
-        name="down_grad",
-    )
-    grad_down_pair = lax.all_gather(grad_down_away, "hi", axis=0)
     dx_sum = []
     for i in range(2):
         dx_sum += call(
@@ -782,7 +775,6 @@
             [((per_expert, width), BF16)],
             from_experts(dx_sent[i]),
             name="add_dx",
-            after=[grad_down_away] if i else [],
         )
     y_sent = call(
         functools.partial(expert_out_kernel, (2 * low, 1)),
@@ -792,6 +784,14 @@
         after=[dx_sum[1]],
     )
     dx_swapped = permute_xor(dx_sum[1], "dp", low)
+    grad_down, grad_down_away = call(
+        functools.partial(down_grad_kernel, 2 * low),
+        [((width, ff), F32), ((width, ff), BF16)],
+        [item for one in saved for item in (one[0], one[1], one[4])],
+        name="down_grad",
+        after=[y_sent[0]],
+    )
+    grad_down_pair = lax.all_gather(grad_down_away, "hi", axis=0)
     ret_dx = [
         swap_seq(item.reshape(seq, cp, width)).reshape(per_expert, width)
         for item in (dx_sum[0], dx_swapped)
@@ -810,7 +810,7 @@
         ret_dx
         + [x1, probs, ids_flat, slot_cols, cot_flat, w_small, gain_second],
         name="back",
-        after=[y_sent[0]],
+        after=[y_sent[0], grad_down_away],
     )
     do_all = swap_seq(do_send).reshape(length, width_h)
 
@@ -916,7 +916,7 @@
         cols_got + small_got,
         scratch=[pltpu.VMEM((width // dp, cols + small_cols), F32)],
         name="merge",
-        after=dx_parts[1:],
+        after=dx_parts[1:] + [grad_up],
     )
     both_up, both_down = call(
         functools.partial(both_experts_kernel, None),

time: 408 us -> 400 us (0.980)
  waiting for transfers between devices: 134 us -> 119 us
  starting transfers between devices: 79.5 us -> 86.3 us
    ppermute x32, waiting for transfers between devices: 87.9 us -> 61.5 us  [permute_xor(): return lax.ppermute(value, axis, [(i, i ^ offset) for i in range(count)])]
    all_to_all x9, waiting for transfers between devices: 46 us -> 57.8 us  [swap_seq(): return lax.all_to_all(value, 'seq', split_axis=0, concat_axis=0, tiled=True)]
    ppermute x32, starting transfers between devices: 36.8 us -> 42 us  [permute_xor(): return lax.ppermute(value, axis, [(i, i ^ offset) for i in range(count)])]
    unnamed x103 -> x107, local copies, waits for them, and re-layouts: 13.2 us -> 13.7 us
  transfers between devices with their start and end apart: 45 -> 45, of which waited for: 16 -> 14; matrix products, arithmetic and copies ran while one was open for 6% -> 6% of each run, Pallas kernels for 33% -> 33%
where the time goes in v1:
time: 400 us; the launch traced here: 395 us
  Pallas kernels  134 us (34%)
  waiting for transfers between devices  119 us (30%)
  starting transfers between devices  86.3 us (22%)
  local copies, waits for them, and re-layouts  37 us (9%)
  between operations  14.7 us (4%)
    pallas_call x25, Pallas kernels, call(): pl.pallas_call(body, out_shape=[jax.ShapeDtypeStruct(s, d) for s, d in ou...  134 us
    ppermute x32, waiting for transfers between devices, permute_xor(): return lax.ppermute(value, axis, [(i, i ^ offset) for i in range(count)])  61.5 us
    all_to_all x9, waiting for transfers between devices, swap_seq(): return lax.all_to_all(value, 'seq', split_axis=0, concat_axis=0, tiled=True)  57.8 us
    all_to_all x9, starting transfers between devices, swap_seq(): return lax.all_to_all(value, 'seq', split_axis=0, concat_axis=0, tiled=True)  43.6 us
    ppermute x32, starting transfers between devices, permute_xor(): return lax.ppermute(value, axis, [(i, i ^ offset) for i in range(count)])  42 us
    unnamed x107, local copies, waits for them, and re-layouts  13.7 us
  transfers between devices with their start and end apart: 45, of which 14 were waited for; matrix products, arithmetic and copies ran while one was open for 6% of the time, Pallas kernels for 33%

profile of v1, /device:TPU:0, one launch (start us, length us, event | category | flops | bytes accessed | tf_op | source)
XLA Modules:
  0.0 395.3 jit_solution(15676668178328484614)
XLA Ops:
  13.2 6.3 %all-to-all-start = ((bf16[8,24,640]{2,1,0:T(8,128)(2,1)}), bf16[8,24,640]{2,1,0:T(8,128)(2,1)S(1)}, u32[]{:S(2)}, u32[]{:S(2)}) async-start(bf16[8,24,640]{2,1,0:T(8,128)(2,1)} %bitcast.10), calls=%async_computation | async-start | bytes 491520 | tf_op jit(solution)/shard_map/all_to_all | solution.py:607
  21.6 2.4 collective-permute-start.1
  24.1 11.4 %collective-permute-done.refs_3_.refs_2_ = bf16[128,768]{1,0:T(8,128)(2,1)S(1)} collective-permute-done((bf16[128,768]{1,0:T(8,128)(2,1)S(1)}, bf16[128,768]{1,0:T(8,128)(2,1)S(1)}, u32[]{:S(2)}, u32[]{:S(2)}) %collective-permute-start) | collective-permute-done | bytes 196640 | tf_op jit(solution)/shard_map/ppermute | solution.py:599
  37.1 5.8 %collective-permute-done.1.refs_4_.refs_3_ = bf16[128,768]{1,0:T(8,128)(2,1)S(1)} collective-permute-done((bf16[128,768]{1,0:T(8,128)(2,1)S(1)}, bf16[128,768]{1,0:T(8,128)(2,1)S(1)}, u32[]{:S(2)}, u32[]{:S(2)}) %collective-permute-start.1) | collective-permute-done | bytes 196640 | tf_op jit(solution)/shard_map/ppermute | solution.py:599
  47.9 5.8 %collective-permute-done.8.refs_12_.refs_11_ = bf16[192,640]{1,0:T(8,128)(2,1)S(1)} collective-permute-done((bf16[192,640]{1,0:T(8,128)(2,1)S(1)}, bf16[192,640]{1,0:T(8,128)(2,1)S(1)}, u32[]{:S(2)}, u32[]{:S(2)}) %collective-permute-start.8) | collective-permute-done | bytes 245792 | tf_op jit(solution)/shard_map/ppermute | solution.py:599
  54.5 3.6 route.1
  58.2 5.1 %all-to-all-start.2 = ((bf16[8,80,768]{2,1,0:T(8,128)(2,1)}), bf16[8,80,768]{2,1,0:T(8,128)(2,1)S(1)}, u32[]{:S(2)}, u32[]{:S(2)}) async-start(bf16[8,80,768]{2,1,0:T(8,128)(2,1)} %bitcast.81), calls=%async_computation.2 | async-start | bytes 1966080 | tf_op jit(solution)/shard_map/all_to_all | solution.py:607
  63.5 3.7 constant_dynamic-slice_fusion
  72.6 11.7 %attn_fwd.1 = (bf16[1024,192]{1,0:T(8,128)(2,1)}, bf16[1024,640]{1,0:T(8,128)(2,1)}, bf16[1024,768]{1,0:T(8,128)(2,1)}, bf16[768,640]{1,0:T(8,128)(2,1)}, f32[10...) custom-call(s32[5]{0:T(128)} %stack.28.refs_0_, bf16[128,768]{1,0:T(8,128)(2,1)} %copy-done.18, ...), custom_call_target="tpu_custom_call" | custom-call | bytes 1 | tf_op jit(solution)/shard_map/attn_fwd/pallas_call | solution.py:55
  86.4 5.8 %all-to-all-done.2 = bf16[8,80,768]{2,1,0:T(8,128)(2,1)S(1)} async-done(((bf16[8,80,768]{2,1,0:T(8,128)(2,1)}), bf16[8,80,768]{2,1,0:T(8,128)(2,1)S(1)}, u32[]{:S(2)}, u32[]{:S(2)}) %all-to-all-start.2) | async-done | bytes 983072 | tf_op jit(solution)/shard_map/all_to_all | solution.py:607
  92.1 3.5 all-to-all-start.1
  97.2 10.8 %all-to-all-done.1 = bf16[8,128,192]{1,2,0:T(8,128)(2,1)S(1)} async-done(((bf16[8,128,192]{1,2,0:T(8,128)(2,1)}), bf16[8,128,192]{1,2,0:T(8,128)(2,1)S(1)}, u32[]{:S(2)}, u32[]{:S(2)}) %all-to-all-start.1) | async-done | bytes 393248 | tf_op jit(solution)/shard_map/all_to_all | solution.py:607
  110.1 4.7 %mid.1 = (f32[256,768]{1,0:T(8,128)}, bf16[256,768]{1,0:T(8,128)(2,1)}, f32[256,16]{1,0:T(8,128)}, f32[1,768]{1,0:T(1,128)}, bf16[640,768]{1,0:T(8,128)(2,1)}) custom-call(bf16[8,128,192]{2,1,0:T(8,128)(2,1)} %copy.50.refs_0_.refs_1_, bf16[256,768]{1,0:T(8,128)(2,1)} %bitcast.74, s32[256,2]{1,0:T(8,128)} %bitcast.84, ...), custom_call_target="tpu_custom_call" | custom-call | bytes 1 | tf_op jit(solution)/shard_map/mid/pallas_call | solution.py:55
  114.8 5.2 %all-to-all-start.3 = ((bf16[8,80,768]{2,1,0:T(8,128)(2,1)}), bf16[8,80,768]{2,1,0:T(8,128)(2,1)S(1)}, u32[]{:S(2)}, u32[]{:S(2)}) async-start(bf16[8,80,768]{2,1,0:T(8,128)(2,1)} %bitcast.107), calls=%async_computation.3 | async-start | bytes 1966080 | tf_op jit(solution)/shard_map/all_to_all | solution.py:607
  121.6 23.6 %all-to-all-done.3 = bf16[8,80,768]{2,1,0:T(8,128)(2,1)S(1)} async-done(((bf16[8,80,768]{2,1,0:T(8,128)(2,1)}), bf16[8,80,768]{2,1,0:T(8,128)(2,1)S(1)}, u32[]{:S(2)}, u32[]{:S(2)}) %all-to-all-start.3) | async-done | bytes 983072 | tf_op jit(solution)/shard_map/all_to_all | solution.py:607
  148.8 17.4 %collective-permute-done.12.refs_0_.refs_2_ = bf16[320,768]{1,0:T(8,128)(2,1)S(1)} collective-permute-done((bf16[320,768]{1,0:T(8,128)(2,1)S(1)}, bf16[320,768]{1,0:T(8,128)(2,1)S(1)}, u32[]{:S(2)}, u32[]{:S(2)}) %collective-permute-start.12) | collective-permute-done | bytes 491552 | tf_op jit(solution)/shard_map/ppermute | solution.py:599
  167.7 3.2 dynamic-slice_bitcast_fusion
  171.7 6.4 %expert.5 = (bf16[320,768]{1,0:T(8,128)(2,1)}, bf16[320,768]{1,0:T(8,128)(2,1)}, bf16[320,768]{1,0:T(8,128)(2,1)}, bf16[320,768]{1,0:T(8,128)(2,1)}, bf16[320,768]{1,0:T(8,128)(2,1)}, /*index=5*/bf16[320,768]{1,0:T(8,128)(2,1)}) custom-call(bf16[320,768]{1,0:T(8,128)(2,1)} %copy-done.6, bf16[320,768]{1,0:T(8,128)(2,1)} %copy-done.13, ...), custom_call_target="tpu_custom_call" | custom-call | bytes 1 | tf_op jit(solution)/shard_map/expert/pallas_call | solution.py:55
  181.2 6.4 %expert.7 = (bf16[320,768]{1,0:T(8,128)(2,1)}, bf16[320,768]{1,0:T(8,128)(2,1)}, bf16[320,768]{1,0:T(8,128)(2,1)}, bf16[320,768]{1,0:T(8,128)(2,1)}, bf16[320,768]{1,0:T(8,128)(2,1)}, /*index=5*/bf16[320,768]{1,0:T(8,128)(2,1)}) custom-call(bf16[320,768]{1,0:T(8,128)(2,1)} %copy-done.7, bf16[320,768]{1,0:T(8,128)(2,1)} %copy-done.35, ...), custom_call_target="tpu_custom_call" | custom-call | bytes 1 | tf_op jit(solution)/shard_map/expert/pallas_call | solution.py:55
  187.6 2.4 collective-permute-start.16
  190.0 6.4 %expert.4 = (bf16[320,768]{1,0:T(8,128)(2,1)}, bf16[320,768]{1,0:T(8,128)(2,1)}, bf16[320,768]{1,0:T(8,128)(2,1)}, bf16[320,768]{1,0:T(8,128)(2,1)}, bf16[320,768]{1,0:T(8,128)(2,1)}, /*index=5*/bf16[320,768]{1,0:T(8,128)(2,1)}) custom-call(bf16[320,768]{1,0:T(8,128)(2,1)} %bitcast.71, bf16[320,768]{1,0:T(8,128)(2,1)} %bitcast.78, ...), custom_call_target="tpu_custom_call" | custom-call | bytes 1 | tf_op jit(solution)/shard_map/expert/pallas_call | solution.py:55
  199.4 3.5 all-to-all-start.4
  203.1 6.4 %expert.6 = (bf16[320,768]{1,0:T(8,128)(2,1)}, bf16[320,768]{1,0:T(8,128)(2,1)}, bf16[320,768]{1,0:T(8,128)(2,1)}, bf16[320,768]{1,0:T(8,128)(2,1)}, bf16[320,768]{1,0:T(8,128)(2,1)}, /*index=5*/bf16[320,768]{1,0:T(8,128)(2,1)}) custom-call(bf16[320,768]{1,0:T(8,128)(2,1)} %copy-done.5, bf16[320,768]{1,0:T(8,128)(2,1)} %copy-done.34, ...), custom_call_target="tpu_custom_call" | custom-call | bytes 1 | tf_op jit(solution)/shard_map/expert/pallas_call | solution.py:55
  210.3 2.3 add_dx.2.refs_10_
  213.1 6.8 %expert_out.1 = (bf16[320,768]{1,0:T(8,128)(2,1)}, bf16[320,768]{1,0:T(8,128)(2,1)}, bf16[320,768]{1,0:T(8,128)(2,1)}, bf16[320,768]{1,0:T(8,128)(2,1)}) custom-call(bf16[320,768]{1,0:T(8,128)(2,1)} %get-tuple-element.89.refs_0_, bf16[320,768]{1,0:T(8,128)(2,1)} %get-tuple-element.90.refs_1_, bf16[320,768]{1,0:T(8,128)(2,1)} %get-tuple-element.91.refs_2_.refs_3_, ...), custom_call_target="tpu_custom_call" | custom-call | bytes 1 | tf_op jit(solution)/shard_map/expert_out/pallas_call | solution.py:55
  219.9 9.3 %down_grad.1 = (f32[768,768]{1,0:T(8,128)}, bf16[768,768]{1,0:T(8,128)(2,1)}) custom-call(bf16[320,768]{1,0:T(8,128)(2,1)} %get-tuple-element.89.refs_0_, bf16[320,768]{1,0:T(8,128)(2,1)} %get-tuple-element.90.refs_1_, bf16[320,768]{1,0:T(8,128)(2,1)} %get-tuple-element.108.refs_2_, bf16[320,768]{1,0:T(8,128)(2,1)} %get-tuple-element.91.refs_2_.refs_3_, ...), custom_call_target="tpu_custom_call" | custom-call | bytes 1 | tf_op jit(solution)/shard_map/down_grad/pallas_call | solution.py:55
  229.3 5.1 %all-to-all-start.5 = ((bf16[8,40,768]{2,1,0:T(8,128)(2,1)}), bf16[8,40,768]{2,1,0:T(8,128)(2,1)S(1)}, u32[]{:S(2)}, u32[]{:S(2)}) async-start(bf16[8,40,768]{2,1,0:T(8,128)(2,1)} %bitcast.33), calls=%async_computation.5 | async-start | bytes 983040 | tf_op jit(solution)/shard_map/all_to_all | solution.py:607
  236.5 12.6 %all-to-all-done.5 = bf16[8,40,768]{2,1,0:T(8,128)(2,1)S(1)} async-done(((bf16[8,40,768]{2,1,0:T(8,128)(2,1)}), bf16[8,40,768]{2,1,0:T(8,128)(2,1)S(1)}, u32[]{:S(2)}, u32[]{:S(2)}) %all-to-all-start.5) | async-done | bytes 491552 | tf_op jit(solution)/shard_map/all_to_all | solution.py:607
  249.9 5.1 %back.1 = (f32[256,768]{1,0:T(8,128)}, bf16[256,768]{1,0:T(8,128)(2,1)}, bf16[8,128,192]{2,1,0:T(8,128)(2,1)}, f32[256,16]{1,0:T(8,128)}, bf16[256,768]{1,0:T(8,128)(2,1)}) custom-call(bf16[320,768]{1,0:T(8,128)(2,1)} %bitcast.97, bf16[320,768]{1,0:T(8,128)(2,1)} %bitcast.99, f32[256,768]{1,0:T(8,128)} %get-tuple-element.105.refs_2_, ...), custom_call_target="tpu_custom_call" | custom-call | bytes 1 | tf_op jit(solution)/shard_map/back/pallas_call | solution.py:55
  257.0 3.5 all-to-all-start.7
  260.4 3.9 small_grad.1
  265.3 2.6 add_y.1
  269.4 12.3 %collective-permute-done.21.refs_8_ = bf16[320,768]{1,0:T(8,128)(2,1)S(1)} collective-permute-done((bf16[320,768]{1,0:T(8,128)(2,1)}, bf16[320,768]{1,0:T(8,128)(2,1)S(1)}, u32[]{:S(2)}, u32[]{:S(2)}) %collective-permute-start.21) | collective-permute-done | bytes 491552 | tf_op jit(solution)/shard_map/ppermute | solution.py:599
  284.6 4.7 %all-to-all-start.6 = ((bf16[8,80,768]{2,1,0:T(8,128)(2,1)}), bf16[8,80,768]{2,1,0:T(8,128)(2,1)S(1)}, u32[]{:S(2)}, u32[]{:S(2)}) async-start(bf16[8,80,768]{2,1,0:T(8,128)(2,1)} %side.1.refs_7_), calls=%async_computation.6 | async-start | bytes 1966080 | tf_op jit(solution)/shard_map/all_to_all | solution.py:607
  289.6 5.7 %up_grad_away.1.refs_8_ = bf16[768,768]{1,0:T(8,128)(2,1)} custom-call(bf16[320,768]{1,0:T(8,128)(2,1)} %bitcast.72, bf16[320,768]{1,0:T(8,128)(2,1)} %copy-done.6, bf16[320,768]{1,0:T(8,128)(2,1)} %copy-done.5, bf16[320,768]{1,0:T(8,128)(2,1)} %copy-done.7, bf16[320,768]{1,0:T(8,128)(2,1)} %get-tuple-element.125.refs_4_, ...), custom_call_target="tpu_custom_call" | custom-call | bytes 1 | tf_op jit(solution)/shard_map/up_grad_away/pallas_call | solution.py:55
  296.4 16.6 %attn_bwd.1 = (bf16[4,128,768]{2,1,0:T(8,128)(2,1)}, bf16[4,128,768]{2,1,0:T(8,128)(2,1)}, bf16[1024,640]{1,0:T(8,128)(2,1)}, f32[8,128]{1,0:T(8,128)}) custom-call(s32[5]{0:T(128)} %stack.28.refs_0_, bf16[1024,192]{1,0:T(8,128)(2,1)} %bitcast.94, bf16[1024,640]{1,0:T(8,128)(2,1)} %get-tuple-element.121.refs_2_, ...), custom_call_target="tpu_custom_call" | custom-call | bytes 1 | tf_op jit(solution)/shard_map/attn_bwd/pallas_call | solution.py:55
  317.9 2.3 pair.1
  321.9 4.6 %cols.1 = (bf16[208,640]{1,0:T(8,128)(2,1)}, bf16[208,640]{1,0:T(8,128)(2,1)}, bf16[208,640]{1,0:T(8,128)(2,1)}, bf16[208,640]{1,0:T(8,128)(2,1)}) custom-call(s32[5]{0:T(128)} %stack.28.refs_0_, bf16[1024,768]{1,0:T(8,128)(2,1)} %get-tuple-element.137.refs_1_, bf16[1024,640]{1,0:T(8,128)(2,1)} %get-tuple-element.138.refs_2_, ...), custom_call_target="tpu_custom_call" | custom-call | bytes 1 | tf_op jit(solution)/shard_map/cols/pallas_call | solution.py:55
  328.2 3.2 collective-permute-done.30.refs_6_
  331.4 6.0 %collective-permute-start.28 = (bf16[208,640]{1,0:T(8,128)(2,1)}, bf16[208,640]{1,0:T(8,128)(2,1)S(1)}, u32[]{:S(2)}, u32[]{:S(2)}) collective-permute-start(bf16[208,640]{1,0:T(8,128)(2,1)} %get-tuple-element.143), channel_id=1, source_target_pairs={{0,24},{8,16},{16,8},{24,0},{1,25},{9,17},{17,9},{25,1},{2,26},{10... | collective-permute-start | bytes 798728 | tf_op jit(solution)/shard_map/ppermute | solution.py:599
  341.1 6.1 %up_grad.1.refs_11_.refs_1_ = f32[768,768]{1,0:T(8,128)} custom-call(bf16[320,768]{1,0:T(8,128)(2,1)} %bitcast.73, bf16[320,768]{1,0:T(8,128)(2,1)} %copy-done.6, bf16[320,768]{1,0:T(8,128)(2,1)} %copy-done.5, bf16[320,768]{1,0:T(8,128)(2,1)} %copy-done.7, bf16[320,768]{1,0:T(8,128)(2,1)} %get-tuple-element.147.refs_4_, ...), custom_call_target="tpu_custom_call" | custom-call | bytes 1 | tf_op jit(solution)/shard_map/up_grad/pallas_call | solution.py:55
  347.2 3.6 collective-permute-done.24.refs_3_.refs_9_
  351.9 2.8 merge.1
  354.7 6.8 %all-to-all-start.8 = ((bf16[8,32,1536]{2,1,0:T(8,128)(2,1)}), bf16[8,32,1536]{2,1,0:T(8,128)(2,1)S(1)}, u32[]{:S(2)}, u32[]{:S(2)}) async-start(bf16[8,32,1536]{2,1,0:T(8,128)(2,1)} %merge.1), calls=%async_computation.8 | async-start | bytes 1572864 | tf_op jit(solution)/shard_map/all_to_all | solution.py:607
  362.2 2.8 last.1.refs_3_
  366.0 3.3 mixed.1.refs_4_
  369.4 8.0 %both_experts.1 = (f32[2,768,768]{2,1,0:T(8,128)}, f32[2,768,768]{2,1,0:T(8,128)}) custom-call(s32[5]{0:T(128)} %stack.28.refs_0_, f32[768,768]{1,0:T(8,128)} %up_grad.1.refs_11_.refs_1_, bf16[2,768,768]{2,1,0:T(8,128)(2,1)} %bitcast.88, f32[768,768]{1,0:T(8,128)} %get-tuple-element.151.refs_3_, bf16[2,768,768]{2,1,0:T(8,128)(2,1)} %bitcast.87), custom_call_target="tpu_custom_call" | custom-call | bytes 1 | tf_op jit(solution)/shard_map/both_experts/pallas_call | solution.py:55
  377.4 5.1 %all-to-all-done.8.refs_0_ = bf16[8,32,1536]{2,1,0:T(8,128)(2,1)S(1)} async-done(((bf16[8,32,1536]{2,1,0:T(8,128)(2,1)}), bf16[8,32,1536]{2,1,0:T(8,128)(2,1)S(1)}, u32[]{:S(2)}, u32[]{:S(2)}) %all-to-all-start.8) | async-done | bytes 786464 | tf_op jit(solution)/shard_map/all_to_all | solution.py:607
  (210 shorter events, 73.9 us)
Async XLA Ops:
  7.2 61.7 %copy-start = (bf16[32,12]{0,1:T(8,128)(2,1)S(1)}, bf16[32,12]{0,1:T(8,128)(2,1)}, u32[]{:S(2)}) copy-start(bf16[32,12]{0,1:T(8,128)(2,1)} %param.18) | copy-start | bytes 2308
  7.2 101.9 %all-gather.8.cloned.1.call-start = ((), (), s32[]{:S(2)}) async-start(), calls=%async_computation.9 | async-start | bytes 1419264 | tf_op jit(solution)/shard_map/all_gather | solution.py:674
  12.4 34.0 %copy-start.43 = (s32[2,1,128,2]{2,3,1,0:T(2,128)S(1)}, s32[2,1,128,2]{2,3,1,0:T(2,128)}, u32[]{:S(2)}) copy-start(s32[2,1,128,2]{2,3,1,0:T(2,128)} %param.14) | copy-start | bytes 6148
  13.2 22.4 %all-to-all-start = ((bf16[8,24,640]{2,1,0:T(8,128)(2,1)}), bf16[8,24,640]{2,1,0:T(8,128)(2,1)S(1)}, u32[]{:S(2)}, u32[]{:S(2)}) async-start(bf16[8,24,640]{2,1,0:T(8,128)(2,1)} %bitcast.10), calls=%async_computation | async-start | bytes 491520 | tf_op jit(solution)/shard_map/all_to_all | solution.py:607
  19.6 38.6 %copy-start.18 = (bf16[128,768]{1,0:T(8,128)(2,1)}, bf16[128,768]{1,0:T(8,128)(2,1)S(1)}, u32[]{:S(2)}) copy-start(bf16[128,768]{1,0:T(8,128)(2,1)S(1)} %get-tuple-element.205.refs_1_) | copy-start | bytes 589828
  19.6 15.9 %collective-permute-start = (bf16[128,768]{1,0:T(8,128)(2,1)S(1)}, bf16[128,768]{1,0:T(8,128)(2,1)S(1)}, u32[]{:S(2)}, u32[]{:S(2)}) collective-permute-start(bf16[128,768]{1,0:T(8,128)(2,1)S(1)} %get-tuple-element.204), channel_id=1, source_target_pairs={{0,2},{1,3},{2,0},{3,1},{4,6},{5,7},{6,4},{7,5},{8,10},{9,11},{10,... | collective-permute-start | bytes 589832 | tf_op jit(solution)/shard_map/ppermute | solution.py:599
  21.6 21.3 %collective-permute-start.1 = (bf16[128,768]{1,0:T(8,128)(2,1)S(1)}, bf16[128,768]{1,0:T(8,128)(2,1)S(1)}, u32[]{:S(2)}, u32[]{:S(2)}) collective-permute-start(bf16[128,768]{1,0:T(8,128)(2,1)S(1)} %get-tuple-element.203), channel_id=1, source_target_pairs={{0,4},{1,5},{2,6},{3,7},{4,0},{5,1},{6,2},{7,3},{8,12},{9,13},{10,... | collective-permute-start | bytes 589832 | tf_op jit(solution)/shard_map/ppermute | solution.py:599
  24.0 20.4 %collective-permute-start.2 = (bf16[128,768]{1,0:T(8,128)(2,1)S(1)}, bf16[128,768]{1,0:T(8,128)(2,1)S(1)}, u32[]{:S(2)}, u32[]{:S(2)}) collective-permute-start(bf16[128,768]{1,0:T(8,128)(2,1)S(1)} %get-tuple-element.202), channel_id=1, source_target_pairs={{0,6},{1,7},{2,4},{3,5},{4,2},{5,3},{6,0},{7,1},{8,14},{9,15},{10,... | collective-permute-start | bytes 589832 | tf_op jit(solution)/shard_map/ppermute | solution.py:599
  24.1 21.8 %collective-permute-start.3 = (bf16[128,768]{1,0:T(8,128)(2,1)S(1)}, bf16[128,768]{1,0:T(8,128)(2,1)S(1)}, u32[]{:S(2)}, u32[]{:S(2)}) collective-permute-start(bf16[128,768]{1,0:T(8,128)(2,1)S(1)} %get-tuple-element.205.refs_1_), channel_id=1, source_target_pairs={{0,1},{1,0},{2,3},{3,2},{4,5},{5,4},{6,7},{7,6},{8,9},{9,8},{10,11... | collective-permute-start | bytes 589832 | tf_op jit(solution)/shard_map/ppermute | solution.py:599
  35.5 10.4 %collective-permute-start.4 = (bf16[128,768]{1,0:T(8,128)(2,1)S(1)}, bf16[128,768]{1,0:T(8,128)(2,1)S(1)}, u32[]{:S(2)}, u32[]{:S(2)}) collective-permute-start(bf16[128,768]{1,0:T(8,128)(2,1)S(1)} %collective-permute-done.refs_3_.refs_2_), channel_id=1, source_target_pairs={{0,1},{1,0},{2,3},{3,2},{4,5},{5,4},{6,7},{7,6},{8,9},{9,8},{10,11... | collective-permute-start | bytes 589832 | tf_op jit(solution)/shard_map/ppermute | solution.py:599
  35.5 12.4 %collective-permute-start.7 = (bf16[192,640]{1,0:T(8,128)(2,1)S(1)}, bf16[192,640]{1,0:T(8,128)(2,1)S(1)}, u32[]{:S(2)}, u32[]{:S(2)}) collective-permute-start(bf16[192,640]{1,0:T(8,128)(2,1)S(1)} %bitcast.89), channel_id=1, source_target_pairs={{0,8},{8,0},{16,24},{24,16},{1,9},{9,1},{17,25},{25,17},{2,10},{10... | collective-permute-start | bytes 737288 | tf_op jit(solution)/shard_map/ppermute | solution.py:599
  42.9 10.8 %collective-permute-start.8 = (bf16[192,640]{1,0:T(8,128)(2,1)S(1)}, bf16[192,640]{1,0:T(8,128)(2,1)S(1)}, u32[]{:S(2)}, u32[]{:S(2)}) collective-permute-start(bf16[192,640]{1,0:T(8,128)(2,1)S(1)} %bitcast.90), channel_id=1, source_target_pairs={{0,16},{8,24},{16,0},{24,8},{1,17},{9,25},{17,1},{25,9},{2,18},{10... | collective-permute-start | bytes 737288 | tf_op jit(solution)/shard_map/ppermute | solution.py:599
  44.4 9.3 %collective-permute-start.9 = (bf16[192,640]{1,0:T(8,128)(2,1)S(1)}, bf16[192,640]{1,0:T(8,128)(2,1)S(1)}, u32[]{:S(2)}, u32[]{:S(2)}) collective-permute-start(bf16[192,640]{1,0:T(8,128)(2,1)S(1)} %bitcast.91), channel_id=1, source_target_pairs={{0,24},{8,16},{16,8},{24,0},{1,25},{9,17},{17,9},{25,1},{2,26},{10... | collective-permute-start | bytes 737288 | tf_op jit(solution)/shard_map/ppermute | solution.py:599
  45.9 2.0 collective-permute-start.5
  45.9 2.0 collective-permute-start.6
  58.2 33.9 %all-to-all-start.2 = ((bf16[8,80,768]{2,1,0:T(8,128)(2,1)}), bf16[8,80,768]{2,1,0:T(8,128)(2,1)S(1)}, u32[]{:S(2)}, u32[]{:S(2)}) async-start(bf16[8,80,768]{2,1,0:T(8,128)(2,1)} %bitcast.81), calls=%async_computation.2 | async-start | bytes 1966080 | tf_op jit(solution)/shard_map/all_to_all | solution.py:607
  63.2 104.5 %all-gather.10.cloned.1.call-start = ((), (), s32[]{:S(2)}) async-start(), calls=%async_computation.10 | async-start | bytes 7077888 | tf_op jit(solution)/shard_map/all_gather | solution.py:716
  92.1 15.9 %all-to-all-start.1 = ((bf16[8,128,192]{1,2,0:T(8,128)(2,1)}), bf16[8,128,192]{1,2,0:T(8,128)(2,1)S(1)}, u32[]{:S(2)}, u32[]{:S(2)}) async-start(bf16[8,128,192]{1,2,0:T(8,128)(2,1)} %copy.47), calls=%async_computation.1 | async-start | bytes 786432 | tf_op jit(solution)/shard_map/all_to_all | solution.py:607
  95.7 13.6 %collective-permute-start.10 = (bf16[320,768]{1,0:T(8,128)(2,1)S(1)}, bf16[320,768]{1,0:T(8,128)(2,1)S(1)}, u32[]{:S(2)}, u32[]{:S(2)}) collective-permute-start(bf16[320,768]{1,0:T(8,128)(2,1)S(1)} %bitcast.76), channel_id=1, source_target_pairs={{0,8},{8,0},{16,24},{24,16},{1,9},{9,1},{17,25},{25,17},{2,10},{10... | collective-permute-start | bytes 1474568 | tf_op jit(solution)/shard_map/ppermute | solution.py:599
  114.8 30.3 %all-to-all-start.3 = ((bf16[8,80,768]{2,1,0:T(8,128)(2,1)}), bf16[8,80,768]{2,1,0:T(8,128)(2,1)S(1)}, u32[]{:S(2)}, u32[]{:S(2)}) async-start(bf16[8,80,768]{2,1,0:T(8,128)(2,1)} %bitcast.107), calls=%async_computation.3 | async-start | bytes 1966080 | tf_op jit(solution)/shard_map/all_to_all | solution.py:607
  120.0 28.3 %collective-permute-start.13 = (bf16[320,768]{1,0:T(8,128)(2,1)S(1)}, bf16[320,768]{1,0:T(8,128)(2,1)S(1)}, u32[]{:S(2)}, u32[]{:S(2)}) collective-permute-start(bf16[320,768]{1,0:T(8,128)(2,1)S(1)} %bitcast.110), channel_id=1, source_target_pairs={{0,16},{8,24},{16,0},{24,8},{1,17},{9,25},{17,1},{25,9},{2,18},{10... | collective-permute-start | bytes 1474568 | tf_op jit(solution)/shard_map/ppermute | solution.py:599
  145.2 21.0 %collective-permute-start.12 = (bf16[320,768]{1,0:T(8,128)(2,1)S(1)}, bf16[320,768]{1,0:T(8,128)(2,1)S(1)}, u32[]{:S(2)}, u32[]{:S(2)}) collective-permute-start(bf16[320,768]{1,0:T(8,128)(2,1)S(1)} %bitcast.111), channel_id=1, source_target_pairs={{0,16},{8,24},{16,0},{24,8},{1,17},{9,25},{17,1},{25,9},{2,18},{10... | collective-permute-start | bytes 1474568 | tf_op jit(solution)/shard_map/ppermute | solution.py:599
  146.8 24.1 %collective-permute-start.11 = (bf16[320,768]{1,0:T(8,128)(2,1)S(1)}, bf16[320,768]{1,0:T(8,128)(2,1)S(1)}, u32[]{:S(2)}, u32[]{:S(2)}) collective-permute-start(bf16[320,768]{1,0:T(8,128)(2,1)S(1)} %bitcast.70), channel_id=1, source_target_pairs={{0,8},{8,0},{16,24},{24,16},{1,9},{9,1},{17,25},{25,17},{2,10},{10... | collective-permute-start | bytes 1474568 | tf_op jit(solution)/shard_map/ppermute | solution.py:599
  148.3 30.3 %collective-permute-start.15 = (bf16[320,768]{1,0:T(8,128)(2,1)S(1)}, bf16[320,768]{1,0:T(8,128)(2,1)S(1)}, u32[]{:S(2)}, u32[]{:S(2)}) collective-permute-start(bf16[320,768]{1,0:T(8,128)(2,1)S(1)} %collective-permute-done.13.refs_1_), channel_id=1, source_target_pairs={{0,8},{8,0},{16,24},{24,16},{1,9},{9,1},{17,25},{25,17},{2,10},{10... | collective-permute-start | bytes 1474568 | tf_op jit(solution)/shard_map/ppermute | solution.py:599
  166.2 14.1 %collective-permute-start.14 = (bf16[320,768]{1,0:T(8,128)(2,1)S(1)}, bf16[320,768]{1,0:T(8,128)(2,1)S(1)}, u32[]{:S(2)}, u32[]{:S(2)}) collective-permute-start(bf16[320,768]{1,0:T(8,128)(2,1)S(1)} %collective-permute-done.12.refs_0_.refs_2_), channel_id=1, source_target_pairs={{0,8},{8,0},{16,24},{24,16},{1,9},{9,1},{17,25},{25,17},{2,10},{10... | collective-permute-start | bytes 1474568 | tf_op jit(solution)/shard_map/ppermute | solution.py:599
  178.1 18.3 %collective-permute-start.19 = (bf16[320,768]{1,0:T(8,128)(2,1)}, bf16[320,768]{1,0:T(8,128)(2,1)S(1)}, u32[]{:S(2)}, u32[]{:S(2)}) collective-permute-start(bf16[320,768]{1,0:T(8,128)(2,1)} %get-tuple-element.104), channel_id=1, source_target_pairs={{0,8},{8,0},{16,24},{24,16},{1,9},{9,1},{17,25},{25,17},{2,10},{10... | collective-permute-start | bytes 1474568 | tf_op jit(solution)/shard_map/ppermute | solution.py:599
  187.6 21.9 %collective-permute-start.16 = (bf16[320,768]{1,0:T(8,128)(2,1)}, bf16[320,768]{1,0:T(8,128)(2,1)S(1)}, u32[]{:S(2)}, u32[]{:S(2)}) collective-permute-start(bf16[320,768]{1,0:T(8,128)(2,1)} %get-tuple-element.98), channel_id=1, source_target_pairs={{0,8},{8,0},{16,24},{24,16},{1,9},{9,1},{17,25},{25,17},{2,10},{10... | collective-permute-start | bytes 1474568 | tf_op jit(solution)/shard_map/ppermute | solution.py:599
  199.4 29.9 %all-to-all-start.4 = ((bf16[8,40,768]{2,1,0:T(8,128)(2,1)}), bf16[8,40,768]{2,1,0:T(8,128)(2,1)S(1)}, u32[]{:S(2)}, u32[]{:S(2)}) async-start(bf16[8,40,768]{2,1,0:T(8,128)(2,1)} %bitcast.98), calls=%async_computation.4 | async-start | bytes 983040 | tf_op jit(solution)/shard_map/all_to_all | solution.py:607
  202.9 166.5 %all-gather.14.cloned.1.call-start = ((), (), s32[]{:S(2)}) async-start(), calls=%async_computation.12 | async-start | bytes 3538944 | tf_op jit(solution)/shard_map/all_gather | solution.py:794
  212.5 16.8 %collective-permute-start.20 = (bf16[320,768]{1,0:T(8,128)(2,1)}, bf16[320,768]{1,0:T(8,128)(2,1)}, u32[]{:S(2)}, u32[]{:S(2)}) collective-permute-start(bf16[320,768]{1,0:T(8,128)(2,1)} %add_dx.2.refs_10_), channel_id=1, source_target_pairs={{0,16},{8,24},{16,0},{24,8},{1,17},{9,25},{17,1},{25,9},{2,18},{10... | collective-permute-start | bytes 1474568 | tf_op jit(solution)/shard_map/ppermute | solution.py:599
  229.3 19.8 %all-to-all-start.5 = ((bf16[8,40,768]{2,1,0:T(8,128)(2,1)}), bf16[8,40,768]{2,1,0:T(8,128)(2,1)S(1)}, u32[]{:S(2)}, u32[]{:S(2)}) async-start(bf16[8,40,768]{2,1,0:T(8,128)(2,1)} %bitcast.33), calls=%async_computation.5 | async-start | bytes 983040 | tf_op jit(solution)/shard_map/all_to_all | solution.py:607
  234.4 29.9 %collective-permute-start.17 = (bf16[320,768]{1,0:T(8,128)(2,1)S(1)}, bf16[320,768]{1,0:T(8,128)(2,1)S(1)}, u32[]{:S(2)}, u32[]{:S(2)}) collective-permute-start(bf16[320,768]{1,0:T(8,128)(2,1)S(1)} %copy-done.46), channel_id=1, source_target_pairs={{0,8},{8,0},{16,24},{24,16},{1,9},{9,1},{17,25},{25,17},{2,10},{10... | collective-permute-start | bytes 1474568 | tf_op jit(solution)/shard_map/ppermute | solution.py:599
  234.5 29.8 %collective-permute-start.18 = (bf16[320,768]{1,0:T(8,128)(2,1)S(1)}, bf16[320,768]{1,0:T(8,128)(2,1)S(1)}, u32[]{:S(2)}, u32[]{:S(2)}) collective-permute-start(bf16[320,768]{1,0:T(8,128)(2,1)S(1)} %copy-done.45), channel_id=1, source_target_pairs={{0,8},{8,0},{16,24},{24,16},{1,9},{9,1},{17,25},{25,17},{2,10},{10... | collective-permute-start | bytes 1474568 | tf_op jit(solution)/shard_map/ppermute | solution.py:599
  257.0 27.6 %all-to-all-start.7 = ((bf16[8,128,192]{1,2,0:T(8,128)(2,1)}), bf16[8,128,192]{1,2,0:T(8,128)(2,1)S(1)}, u32[]{:S(2)}, u32[]{:S(2)}) async-start(bf16[8,128,192]{1,2,0:T(8,128)(2,1)} %copy.54), calls=%async_computation.7 | async-start | bytes 786432 | tf_op jit(solution)/shard_map/all_to_all | solution.py:607
  267.9 13.8 %collective-permute-start.21 = (bf16[320,768]{1,0:T(8,128)(2,1)}, bf16[320,768]{1,0:T(8,128)(2,1)S(1)}, u32[]{:S(2)}, u32[]{:S(2)}) collective-permute-start(bf16[320,768]{1,0:T(8,128)(2,1)} %get-tuple-element.119), channel_id=1, source_target_pairs={{0,16},{8,24},{16,0},{24,8},{1,17},{9,25},{17,1},{25,9},{2,18},{10... | collective-permute-start | bytes 1474568 | tf_op jit(solution)/shard_map/ppermute | solution.py:599
  284.6 70.1 %all-to-all-start.6 = ((bf16[8,80,768]{2,1,0:T(8,128)(2,1)}), bf16[8,80,768]{2,1,0:T(8,128)(2,1)S(1)}, u32[]{:S(2)}, u32[]{:S(2)}) async-start(bf16[8,80,768]{2,1,0:T(8,128)(2,1)} %side.1.refs_7_), calls=%async_computation.6 | async-start | bytes 1966080 | tf_op jit(solution)/shard_map/all_to_all | solution.py:607
  289.4 80.0 %all-gather.12.cloned.1.call-start = ((), (), s32[]{:S(2)}) async-start(), calls=%async_computation.11 | async-start | bytes 3538944 | tf_op jit(solution)/shard_map/all_gather | solution.py:842
  313.0 4.0 %collective-permute-start.22 = (bf16[4,128,768]{2,1,0:T(8,128)(2,1)}, bf16[4,128,768]{2,1,0:T(8,128)(2,1)S(1)}, u32[]{:S(2)}, u32[]{:S(2)}) collective-permute-start(bf16[4,128,768]{2,1,0:T(8,128)(2,1)} %get-tuple-element.130), channel_id=1, source_target_pairs={{0,1},{1,0},{2,3},{3,2},{4,5},{5,4},{6,7},{7,6},{8,9},{9,8},{10,11... | collective-permute-start | bytes 2359304 | tf_op jit(solution)/shard_map/ppermute | solution.py:599
  313.4 13.2 %collective-permute-start.29 = (bf16[192,896]{1,0:T(8,128)(2,1)S(1)}, bf16[192,896]{1,0:T(8,128)(2,1)S(1)}, u32[]{:S(2)}, u32[]{:S(2)}) collective-permute-start(bf16[192,896]{1,0:T(8,128)(2,1)S(1)} %copy-done.49), channel_id=1, source_target_pairs={{0,8},{8,0},{16,24},{24,16},{1,9},{9,1},{17,25},{25,17},{2,10},{10... | collective-permute-start | bytes 1032200 | tf_op jit(solution)/shard_map/ppermute | solution.py:599
  313.6 17.8 %collective-permute-start.30 = (bf16[192,896]{1,0:T(8,128)(2,1)S(1)}, bf16[192,896]{1,0:T(8,128)(2,1)S(1)}, u32[]{:S(2)}, u32[]{:S(2)}) collective-permute-start(bf16[192,896]{1,0:T(8,128)(2,1)S(1)} %copy-done.48), channel_id=1, source_target_pairs={{0,16},{8,24},{16,0},{24,8},{1,17},{9,25},{17,1},{25,9},{2,18},{10... | collective-permute-start | bytes 1032200 | tf_op jit(solution)/shard_map/ppermute | solution.py:599
  315.1 22.2 %collective-permute-start.31 = (bf16[192,896]{1,0:T(8,128)(2,1)S(1)}, bf16[192,896]{1,0:T(8,128)(2,1)S(1)}, u32[]{:S(2)}, u32[]{:S(2)}) collective-permute-start(bf16[192,896]{1,0:T(8,128)(2,1)S(1)} %copy-done.47), channel_id=1, source_target_pairs={{0,24},{8,16},{16,8},{24,0},{1,25},{9,17},{17,9},{25,1},{2,26},{10... | collective-permute-start | bytes 1032200 | tf_op jit(solution)/shard_map/ppermute | solution.py:599
  320.2 19.4 %collective-permute-start.23 = (bf16[128,768]{1,0:T(8,128)(2,1)}, bf16[128,768]{1,0:T(8,128)(2,1)S(1)}, u32[]{:S(2)}, u32[]{:S(2)}) collective-permute-start(bf16[128,768]{1,0:T(8,128)(2,1)} %get-tuple-element.132), channel_id=1, source_target_pairs={{0,2},{1,3},{2,0},{3,1},{4,6},{5,7},{6,4},{7,5},{8,10},{9,11},{10,... | collective-permute-start | bytes 589832 | tf_op jit(solution)/shard_map/ppermute | solution.py:599
  326.4 24.4 %collective-permute-start.26 = (bf16[208,640]{1,0:T(8,128)(2,1)}, bf16[208,640]{1,0:T(8,128)(2,1)S(1)}, u32[]{:S(2)}, u32[]{:S(2)}) collective-permute-start(bf16[208,640]{1,0:T(8,128)(2,1)} %get-tuple-element.141), channel_id=1, source_target_pairs={{0,8},{8,0},{16,24},{24,16},{1,9},{9,1},{17,25},{25,17},{2,10},{10... | collective-permute-start | bytes 798728 | tf_op jit(solution)/shard_map/ppermute | solution.py:599
  326.7 24.2 %collective-permute-start.27 = (bf16[208,640]{1,0:T(8,128)(2,1)}, bf16[208,640]{1,0:T(8,128)(2,1)S(1)}, u32[]{:S(2)}, u32[]{:S(2)}) collective-permute-start(bf16[208,640]{1,0:T(8,128)(2,1)} %get-tuple-element.142), channel_id=1, source_target_pairs={{0,16},{8,24},{16,0},{24,8},{1,17},{9,25},{17,1},{25,9},{2,18},{10... | collective-permute-start | bytes 798728 | tf_op jit(solution)/shard_map/ppermute | solution.py:599
  331.4 19.6 %collective-permute-start.28 = (bf16[208,640]{1,0:T(8,128)(2,1)}, bf16[208,640]{1,0:T(8,128)(2,1)S(1)}, u32[]{:S(2)}, u32[]{:S(2)}) collective-permute-start(bf16[208,640]{1,0:T(8,128)(2,1)} %get-tuple-element.143), channel_id=1, source_target_pairs={{0,24},{8,16},{16,8},{24,0},{1,25},{9,17},{17,9},{25,1},{2,26},{10... | collective-permute-start | bytes 798728 | tf_op jit(solution)/shard_map/ppermute | solution.py:599
  337.3 13.5 %collective-permute-start.24 = (bf16[128,768]{1,0:T(8,128)(2,1)S(1)}, bf16[128,768]{1,0:T(8,128)(2,1)S(1)}, u32[]{:S(2)}, u32[]{:S(2)}) collective-permute-start(bf16[128,768]{1,0:T(8,128)(2,1)S(1)} %copy-done.51), channel_id=1, source_target_pairs={{0,4},{1,5},{2,6},{3,7},{4,0},{5,1},{6,2},{7,3},{8,12},{9,13},{10,... | collective-permute-start | bytes 589832 | tf_op jit(solution)/shard_map/ppermute | solution.py:599
  339.6 11.3 %collective-permute-start.25 = (bf16[128,768]{1,0:T(8,128)(2,1)S(1)}, bf16[128,768]{1,0:T(8,128)(2,1)S(1)}, u32[]{:S(2)}, u32[]{:S(2)}) collective-permute-start(bf16[128,768]{1,0:T(8,128)(2,1)S(1)} %copy-done.50), channel_id=1, source_target_pairs={{0,6},{1,7},{2,4},{3,5},{4,2},{5,3},{6,0},{7,1},{8,14},{9,15},{10,... | collective-permute-start | bytes 589832 | tf_op jit(solution)/shard_map/ppermute | solution.py:599
  354.7 27.8 %all-to-all-start.8 = ((bf16[8,32,1536]{2,1,0:T(8,128)(2,1)}), bf16[8,32,1536]{2,1,0:T(8,128)(2,1)S(1)}, u32[]{:S(2)}, u32[]{:S(2)}) async-start(bf16[8,32,1536]{2,1,0:T(8,128)(2,1)} %merge.1), calls=%async_computation.8 | async-start | bytes 1572864 | tf_op jit(solution)/shard_map/all_to_all | solution.py:607
  (49 other events, 378.3 us)
Sparse Core Ops, SparseCore 0:
  11.5 69.1 all-gather.7
  82.8 81.0 all-gather.9
  229.4 36.4 all-gather.13
  313.6 54.6 all-gather.11
